TPU v7x, 256 devices: a whole 4x4x8 slice. The times are simulated.
256 devices in a mesh: gx: 32 (over y_lo, z, core), gy: 8 (over x, y_hi).
Axes of the slice: x: 4, y: 4 (y_hi: 2, y_lo: 2; y = y_hi * 2 + y_lo), z: 8, core: 2. Of those that a mesh axis runs over, the one named last changes fastest.
Arguments:
- offsets: float32 [3, 128, 320, 128], P(None, 'gx', 'gy'), may hold values from 0 to 16, as said below
- charges: float32 [128, 320, 128], P('gx', 'gy'), may hold values from -4 to 4
- atom_type: int32 [128, 320, 128], P('gx', 'gy'), may hold values from 0 to 15
- type_radius: float32 [16], replicated, may hold values from 1.2 to 2
- type_scale: float32 [16], replicated, may hold values from 0.5 to 0.85
- tile_mask: int32 [128, 320, 25], P('gx', 'gy'), may hold values from 0 to 1, as said below
Outputs:
- born_radius: float32 [128, 320, 128], P('gx', 'gy')
- atom_energy: float32 [128, 320, 128], P('gx', 'gy')
- force: float32 [3, 128, 320, 128], P(None, 'gx', 'gy')
- born_grad: float32 [128, 320, 128], P('gx', 'gy')
Inputs may be any that keep to these rules, and one draw needn't show every extreme that they name: `offsets`: atoms of a block sit on a 4 x 4 x 128/16 lattice of spacing 2 starting at 1, each coordinate moved by at most 0.5; blocks are 8 wide in the first two dimensions. `tile_mask`: entry k of block (u, v) equals entry 24 - k of block (u + k // 5 - 2, v + k % 5 - 2), the grid wrapping in both dimensions, and entry 12 is always 1. In every draw all 160 blocks of some device have all 25 entries 1.
All inputs are finite; a program needn't handle non-finite values.
Results may differ from a plain program's by a relative error of at most 0.0003.
Values sent between devices are 32-bit elements; how exact they have to be, the bound alone decides.
A program may use at most 64 MiB of HBM per device.

v0:
```python
import jax
import jax.numpy as jnp
from jax import lax
from jax.sharding import PartitionSpec as P

dielectric_factor = 1.0 - 1.0 / 78.5
radius_offset = 0.09
block_side = 8.0


def from_behind(value, axis, steps):
    count = lax.axis_size(axis)
    pairs = [(source, (source + steps) % count) for source in range(count)]
    return lax.ppermute(value, axis, pairs)


def padded(array, sides, width):
    for axis, dim in sides:
        count, length = (lax.axis_size(axis), array.shape[dim])
        up = [(i, (i + 1) % count) for i in range(count)]
        down = [(j, i) for i, j in up]
        last = lax.slice_in_dim(array, length - width, length, axis=dim)
        leading = lax.slice_in_dim(array, 0, width, axis=dim)
        before = lax.ppermute(last, axis, up)
        after = lax.ppermute(leading, axis, down)
        array = jnp.concatenate([before, array, after], axis=dim)
    return array


def atom_terms(atom_type, type_radius, type_scale):
    type_hits = (atom_type[..., None] == jnp.arange(type_radius.shape[0], dtype=jnp.int32)).astype(
        jnp.float32
    )
    radius = jnp.sum(type_hits * type_radius, axis=-1)
    inner_radius = radius - radius_offset
    scaled = jnp.sum(type_hits * type_scale, axis=-1) * inner_radius
    return (radius, inner_radius, scaled)


def hct_integral(distance, inner_radius, scaled):
    outer_edge = distance + scaled
    inner_edge = jnp.maximum(inner_radius, jnp.abs(distance - scaled))
    inv_outer = 1.0 / outer_edge
    inv_inner = 1.0 / inner_edge
    gap_sq = inv_outer * inv_outer - inv_inner * inv_inner
    integral = inv_inner - inv_outer + 0.25 * distance * gap_sq
    integral = (
        integral
        + (0.5 * jnp.log(inner_edge * inv_outer) - 0.25 * scaled * scaled * gap_sq) / distance
    )
    integral = integral + jnp.where(
        inner_radius < scaled - distance, 2.0 * (1.0 / inner_radius - inv_inner), 0.0
    )
    return jnp.where(inner_radius < outer_edge, integral, 0.0)


def separation(pos_home, pos_away, shift):
    moved = pos_away + shift[:, :, None]
    separations = pos_home[:, :, :, None] - moved[:, :, None, :]
    return (separations, jnp.sum(separations * separations, axis=0))


def descreen_tile(home, away, shift, on_diagonal, weights):
    separations, dist_sq = separation(home[0], away[0], shift)
    distance = jnp.sqrt(jnp.where(on_diagonal, 1.0, dist_sq))
    first_side = jnp.sum(
        weights * hct_integral(distance, home[1][:, :, None], away[2][:, None, :]), axis=2
    )
    second_side = jnp.sum(
        weights * hct_integral(distance, away[1][:, None, :], home[2][:, :, None]), axis=1
    )
    return (first_side, second_side)


def screen_tile(home, away, shift, weights):
    separations, dist_sq = separation(home[0], away[0], shift)
    radii_prod = home[1][:, :, None] * away[1][:, None, :]
    damping = jnp.exp(-dist_sq / (4.0 * radii_prod))
    inv_length = 1.0 / jnp.sqrt(dist_sq + radii_prod * damping)
    charge_prod = weights * home[2][:, :, None] * away[2][:, None, :]
    energy = -0.5 * dielectric_factor * charge_prod * inv_length
    strength = charge_prod * inv_length * inv_length * inv_length
    pulling = -dielectric_factor * strength * (1.0 - 0.25 * damping)
    stretch = 0.5 * dielectric_factor * strength * damping * (1.0 + dist_sq / (4.0 * radii_prod))
    push = pulling[None] * separations
    first_side = jnp.concatenate(
        [
            jnp.sum(push, axis=3),
            jnp.sum(energy, axis=2)[None],
            jnp.sum(stretch * away[1][:, None, :], axis=2)[None],
        ],
        axis=0,
    )
    second_side = jnp.concatenate(
        [
            -jnp.sum(push, axis=2),
            jnp.sum(energy, axis=1)[None],
            jnp.sum(stretch * home[1][:, :, None], axis=1)[None],
        ],
        axis=0,
    )
    return (first_side, second_side)


def tile_plan(tile_mask):
    block_count = tile_mask.shape[0] * tile_mask.shape[1]
    live_flags = tile_mask.reshape(block_count, 25)
    live_flags = live_flags * (jnp.arange(25, dtype=jnp.int32) >= 12).astype(jnp.int32)[None, :]
    live_flags = live_flags.reshape(-1)
    tile_order = jnp.argsort(1 - live_flags, stable=True)
    return (tile_order, jnp.sum(live_flags))


def tile_geometry(tile_ids, start, live_count, rows_y):
    block_ids = tile_ids // 25
    offset_code = tile_ids % 25
    step_x = offset_code // 5 - 2
    step_y = offset_code % 5 - 2
    home_x = block_ids // rows_y + 2
    home_y = block_ids % rows_y + 2
    slot_width = rows_y + 4
    home_slot = home_x * slot_width + home_y
    away_slot = (home_x + step_x) * slot_width + home_y + step_y
    shift = jnp.stack(
        [
            step_x.astype(jnp.float32) * block_side,
            step_y.astype(jnp.float32) * block_side,
            jnp.zeros(tile_ids.shape, jnp.float32),
        ],
        axis=0,
    )
    valid = (start + jnp.arange(tile_ids.shape[0], dtype=jnp.int32) < live_count).astype(
        jnp.float32
    )
    return (home_slot, away_slot, shift, offset_code == 12, valid)


def spread_rows(slot_ids, slot_count):
    return (slot_ids[:, None] == jnp.arange(slot_count, dtype=jnp.int32)[None, :]).astype(
        jnp.float32
    )


def fold_columns(columns, rows_y):
    folded = columns[:, :, 4 : rows_y + 4]
    folded = folded.at[:, :, 0:2].add(columns[:, :, 0:2])
    folded = folded.at[:, :, rows_y - 2 : rows_y].add(columns[:, :, rows_y + 6 : rows_y + 8])
    return folded


def settle(slot_sums, rows_x, rows_y):
    extended = slot_sums.reshape(slot_sums.shape[0], rows_x + 4, rows_y + 4, slot_sums.shape[-1])
    arriving = from_behind(extended[:, rows_x + 2 : rows_x + 4], "gx", 1)
    middle = extended[:, 2 : rows_x + 2].at[:, 0:2].add(arriving)
    columns = padded(middle, (("gy", 2),), 2)
    return fold_columns(columns, rows_y)


def body(offsets, charges, atom_type, type_radius, type_scale, tile_mask):
    rows_x, rows_y, atoms = charges.shape
    radius, inner_radius, scaled = atom_terms(atom_type, type_radius, type_scale)
    payload = jnp.concatenate([offsets, jnp.stack([inner_radius, scaled, charges])], axis=0)
    widened = padded(payload, (("gy", 2),), 2)
    ahead = from_behind(widened[:, 0:2], "gx", -1)
    extended = jnp.concatenate([jnp.zeros_like(ahead), widened, ahead], axis=1)
    slot_count = (rows_x + 4) * (rows_y + 4)
    atom_flat = extended.reshape(6, slot_count, atoms)
    tile_order, live_count = tile_plan(tile_mask)
    group_size = 2 * rows_y
    tile_total = rows_x * rows_y * 25
    padded_total = -(-tile_total // group_size) * group_size
    tile_order = jnp.concatenate([tile_order, jnp.zeros((padded_total - tile_total,), jnp.int32)])
    turn_count = (live_count + group_size - 1) // group_size
    diagonal = jnp.eye(atoms, dtype=bool)

    def plan_turn(turn_index):
        start = turn_index * group_size
        tile_ids = lax.dynamic_slice_in_dim(tile_order, start, group_size)
        home_slot, away_slot, shift, diagonal_tile, valid = tile_geometry(
            tile_ids, start, live_count, rows_y
        )
        on_diagonal = diagonal_tile[:, None, None] & diagonal[None]
        weights = jnp.where(on_diagonal, 0.0, 1.0) * valid[:, None, None]
        crossing = 1.0 - diagonal_tile.astype(jnp.float32)
        return (home_slot, away_slot, shift, on_diagonal, weights, crossing)

    def descreen_turn(turn_index, totals):
        home_slot, away_slot, shift, on_diagonal, weights, crossing = plan_turn(turn_index)
        near_rows = jnp.take(atom_flat, home_slot, axis=1)
        far_rows = jnp.take(atom_flat, away_slot, axis=1)
        home = (near_rows[0:3], near_rows[3], near_rows[4])
        away = (far_rows[0:3], far_rows[3], far_rows[4])
        first_side, second_side = descreen_tile(home, away, shift, on_diagonal, weights)
        totals = totals + jnp.einsum(
            "gs,gb->sb",
            spread_rows(home_slot, slot_count),
            first_side,
            precision=lax.Precision.HIGHEST,
        )
        totals = totals + jnp.einsum(
            "gs,gb->sb",
            spread_rows(away_slot, slot_count),
            crossing[:, None] * second_side,
            precision=lax.Precision.HIGHEST,
        )
        return totals

    descreen_slots = lax.fori_loop(
        0, turn_count, descreen_turn, jnp.zeros((slot_count, atoms), jnp.float32)
    )
    descreen_sum = settle(descreen_slots[None], rows_x, rows_y)[0]
    descreen_psi = 0.5 * inner_radius * descreen_sum
    born_radius = 1.0 / (
        1.0 / inner_radius
        - jnp.tanh(descreen_psi * (1.0 - 0.8 * descreen_psi + 4.85 * descreen_psi * descreen_psi))
        / radius
    )
    born_wide = padded(born_radius, (("gy", 1),), 2)
    born_next = from_behind(born_wide[0:2], "gx", -1)
    born_ext = jnp.concatenate([jnp.ones_like(born_next), born_wide, born_next], axis=0)
    born_flat = born_ext.reshape(slot_count, atoms)

    def screen_turn(turn_index, totals):
        home_slot, away_slot, shift, on_diagonal, weights, crossing = plan_turn(turn_index)
        near_rows = jnp.take(atom_flat, home_slot, axis=1)
        far_rows = jnp.take(atom_flat, away_slot, axis=1)
        home = (near_rows[0:3], jnp.take(born_flat, home_slot, axis=0), near_rows[5])
        away = (far_rows[0:3], jnp.take(born_flat, away_slot, axis=0), far_rows[5])
        first_side, second_side = screen_tile(home, away, shift, weights)
        totals = totals + jnp.einsum(
            "gs,cgb->csb",
            spread_rows(home_slot, slot_count),
            first_side,
            precision=lax.Precision.HIGHEST,
        )
        totals = totals + jnp.einsum(
            "gs,cgb->csb",
            spread_rows(away_slot, slot_count),
            crossing[None, :, None] * second_side,
            precision=lax.Precision.HIGHEST,
        )
        return totals

    screen_slots = lax.fori_loop(
        0, turn_count, screen_turn, jnp.zeros((5, slot_count, atoms), jnp.float32)
    )
    pair_sum = settle(screen_slots, rows_x, rows_y)
    charge_sq = charges * charges
    force = pair_sum[0:3]
    atom_energy = pair_sum[3] - 0.5 * dielectric_factor * charge_sq / born_radius
    born_grad = pair_sum[4] + 0.5 * dielectric_factor * charge_sq / (born_radius * born_radius)
    return (born_radius, atom_energy, force, born_grad)


def solution(mesh):
    placed = (
        P(None, "gx", "gy", None),
        P("gx", "gy", None),
        P("gx", "gy", None),
        P(),
        P(),
        P("gx", "gy", None),
    )
    return jax.shard_map(
        body,
        mesh=mesh,
        in_specs=placed,
        out_specs=(
            P("gx", "gy", None),
            P("gx", "gy", None),
            P(None, "gx", "gy", None),
            P("gx", "gy", None),
        ),
        check_vma=False,
    )
```

profile of v0, /device:TPU:30, one launch (start us, length us, event | category | flops | bytes accessed | tf_op | source)
XLA Modules:
  0.0 1484.4 jit_solution(14287874645484101647)
XLA Ops:
  0.6 1.7 select_reduce_fusion
  2.3 0.9 pad_maximum_fusion.12
  3.2 1.2 collective-permute-start
  4.4 2.4 collective-permute-start.1
  6.8 1.8 collective-permute-done
  8.6 3.3 collective-permute-done.1
  11.9 1.0 pad_maximum_fusion.1
  12.9 3.3 collective-permute-start.2
  16.2 1.5 multiply_reduce_fusion.3
  18.4 0.9 copy.25
  19.8 5.8 sort.17
  25.6 1.1 pad_maximum_fusion
  27.5 72.3 %while.34 = (s32[]{:T(128)}, f32[352,128]{1,0:T(8,128)S(1)}, s32[]{:T(128)}, s32[4000]{0:T(1024)S(1)}, s32[]{:T(128)}, /*index=5*/f32[6,352,128]{2,0,1:T(8,128)S...) while((s32[]{:T(128)}, f32[352,128]{1,0:T(8,128)S(1)}, ...), condition=%wide.region_8.10_spmd.clone, body=%wide.region_4.9_spmd.clone.sunk | while | flops 177324640 | bytes 15356147 | solution.py:208
  30.5 5.2 multiply_reduce_fusion.6
  35.7 15.1 %fusion.94 = (f32[80,128]{1,0:T(8,128)S(1)}, f32[80,128]{1,0:T(8,128)S(1)}) fusion(f32[80,128,128]{2,1,0:T(8,128)S(1)} %multiply_reduce_fusion.6, f32[80,128]{1,0:T(8,128)S(1)} %get-tuple-element.647, f32[80,128]{1,0:T(8,128)S(1)} %multiply_multiply_fusion.12, f32[80,128]{1,0:T(8,128)S(1)} %bitcast.122, f32[80,128]{1,0:T(8,128)S(1)} %get-tuple-element.649, ...), kind=kLoop, calls=%fused_computation.15.clone.1 | loop fusion | flops 79933440 | bytes 5669264 | tf_op jit(solution)/shard_map/while/body/reduce_sum | solution.py:69
  51.8 0.8 compare_and_fusion.8
  54.6 5.2 multiply_reduce_fusion.6
  59.8 15.1 %fusion.94 = (f32[80,128]{1,0:T(8,128)S(1)}, f32[80,128]{1,0:T(8,128)S(1)}) fusion(f32[80,128,128]{2,1,0:T(8,128)S(1)} %multiply_reduce_fusion.6, f32[80,128]{1,0:T(8,128)S(1)} %get-tuple-element.647, f32[80,128]{1,0:T(8,128)S(1)} %multiply_multiply_fusion.12, f32[80,128]{1,0:T(8,128)S(1)} %bitcast.122, f32[80,128]{1,0:T(8,128)S(1)} %get-tuple-element.649, ...), kind=kLoop, calls=%fused_computation.15.clone.1 | loop fusion | flops 79933440 | bytes 5669264 | tf_op jit(solution)/shard_map/while/body/reduce_sum | solution.py:69
  75.9 0.8 compare_and_fusion.8
  78.7 5.2 multiply_reduce_fusion.6
  83.9 15.1 %fusion.94 = (f32[80,128]{1,0:T(8,128)S(1)}, f32[80,128]{1,0:T(8,128)S(1)}) fusion(f32[80,128,128]{2,1,0:T(8,128)S(1)} %multiply_reduce_fusion.6, f32[80,128]{1,0:T(8,128)S(1)} %get-tuple-element.647, f32[80,128]{1,0:T(8,128)S(1)} %multiply_multiply_fusion.12, f32[80,128]{1,0:T(8,128)S(1)} %bitcast.122, f32[80,128]{1,0:T(8,128)S(1)} %get-tuple-element.649, ...), kind=kLoop, calls=%fused_computation.15.clone.1 | loop fusion | flops 79933440 | bytes 5669264 | tf_op jit(solution)/shard_map/while/body/reduce_sum | solution.py:69
  99.8 45.5 %collective-permute-start.3 = (f32[1,2,44,128]{3,2,1,0:T(8,128)S(1)}, f32[1,2,44,128]{3,2,1,0:T(8,128)S(1)}, u32[]{:S(2)}, u32[]{:S(2)}) collective-permute-start(f32[1,2,44,128]{3,2,1,0:T(8,128)S(1)} %slice.364), channel_id=1, source_target_pairs={{0,8},{8,16},{16,24},{24,32},{32,40},{40,48},{48,56},{56,64},{64,7... | collective-permute-start | bytes 135176 | tf_op jit(solution)/shard_map/ppermute | solution.py:14
  145.4 0.9 collective-permute-done.3
  146.3 515.6 %collective-permute-start.4 = (f32[1,4,2,128]{3,2,1,0:T(2,128)S(1)}, f32[1,4,2,128]{3,2,1,0:T(2,128)S(1)}, u32[]{:S(2)}, u32[]{:S(2)}) collective-permute-start(f32[1,4,2,128]{3,2,1,0:T(2,128)S(1)} %get-tuple-element.518), channel_id=1, source_target_pairs={{0,1},{1,2},{2,3},{3,4},{4,5},{5,6},{6,7},{7,0},{8,9},{9,10},{10,1... | collective-permute-start | bytes 12296 | tf_op jit(solution)/shard_map/ppermute | solution.py:24
  662.2 1.0 collective-permute-done.4
  663.2 6.1 collective-permute-done.5
  669.6 3.5 collective-permute-start.7
  673.1 1.6 collective-permute-done.6
  674.7 2.2 collective-permute-done.7
  677.0 1.7 collective-permute-done.8
  678.9 90.9 %while.35 = (s32[]{:T(128)}, f32[5,352,128]{2,1,0:T(8,128)S(1)}, s32[]{:T(128)}, s32[4000]{0:T(1024)S(1)}, s32[]{:T(128)}, /*index=5*/f32[6,352,128]{2,0,1:T(8,1...) while((s32[]{:T(128)}, f32[5,352,128]{2,1,0:T(8,128)S(1)}, ...), condition=%wide.region_17.20_spmd.clone, body=%wide.region_9.19_spmd.clone.sunk | while | flops 500275808 | bytes 29793180 | solution.py:244
  679.1 0.8 compare_and_fusion.10
  683.5 5.2 fusion.98
  688.7 9.3 multiply_reduce_fusion.7
  698.0 9.9 fusion.99
  709.4 0.8 compare_and_fusion.10
  713.8 5.2 fusion.98
  719.0 9.3 multiply_reduce_fusion.7
  728.3 9.9 fusion.99
  739.7 0.8 compare_and_fusion.10
  744.1 5.2 fusion.98
  749.3 9.3 multiply_reduce_fusion.7
  758.6 9.9 fusion.99
  769.9 60.3 %collective-permute-start.9 = (f32[5,2,44,128]{3,2,1,0:T(8,128)S(1)}, f32[5,2,44,128]{3,2,1,0:T(8,128)S(1)}, u32[]{:S(2)}, u32[]{:S(2)}) collective-permute-start(f32[5,2,44,128]{3,2,1,0:T(8,128)S(1)} %slice.374), channel_id=1, source_target_pairs={{0,8},{8,16},{16,24},{24,32},{32,40},{40,48},{48,56},{56,64},{64,7... | collective-permute-start | bytes 675848 | tf_op jit(solution)/shard_map/ppermute | solution.py:14
  830.3 1.1 collective-permute-done.9
  831.4 644.0 %collective-permute-start.10 = (f32[5,4,2,128]{3,2,1,0:T(2,128)S(1)}, f32[5,4,2,128]{3,2,1,0:T(2,128)S(1)}, u32[]{:S(2)}, u32[]{:S(2)}) collective-permute-start(f32[5,4,2,128]{3,2,1,0:T(2,128)S(1)} %get-tuple-element.514), channel_id=1, source_target_pairs={{0,1},{1,2},{2,3},{3,4},{4,5},{5,6},{6,7},{7,0},{8,9},{9,10},{10,1... | collective-permute-start | bytes 61448 | tf_op jit(solution)/shard_map/ppermute | solution.py:24
  1475.6 1.4 collective-permute-done.10
  1477.0 6.0 collective-permute-done.11
  (205 shorter events, 28.2 us)
Async XLA Ops:
  3.2 5.4 collective-permute-start
  4.4 7.4 collective-permute-start.1
  12.9 12.8 collective-permute-start.2
  99.8 46.4 %collective-permute-start.3 = (f32[1,2,44,128]{3,2,1,0:T(8,128)S(1)}, f32[1,2,44,128]{3,2,1,0:T(8,128)S(1)}, u32[]{:S(2)}, u32[]{:S(2)}) collective-permute-start(f32[1,2,44,128]{3,2,1,0:T(8,128)S(1)} %slice.364), channel_id=1, source_target_pairs={{0,8},{8,16},{16,24},{24,32},{32,40},{40,48},{48,56},{56,64},{64,7... | collective-permute-start | bytes 135176 | tf_op jit(solution)/shard_map/ppermute | solution.py:14
  146.3 517.0 %collective-permute-start.4 = (f32[1,4,2,128]{3,2,1,0:T(2,128)S(1)}, f32[1,4,2,128]{3,2,1,0:T(2,128)S(1)}, u32[]{:S(2)}, u32[]{:S(2)}) collective-permute-start(f32[1,4,2,128]{3,2,1,0:T(2,128)S(1)} %get-tuple-element.518), channel_id=1, source_target_pairs={{0,1},{1,2},{2,3},{3,4},{4,5},{5,6},{6,7},{7,0},{8,9},{9,10},{10,1... | collective-permute-start | bytes 12296 | tf_op jit(solution)/shard_map/ppermute | solution.py:24
  661.9 7.5 collective-permute-start.5
  669.5 813.5 %copy-start = (f32[4,40,128]{2,1,0:T(8,128)}, f32[4,40,128]{2,1,0:T(8,128)S(1)}, u32[]{:S(2)}) copy-start(f32[4,40,128]{2,1,0:T(8,128)S(1)} %broadcast_divide_fusion.2) | copy-start | bytes 245764
  669.5 5.2 collective-permute-start.6
  669.6 7.3 collective-permute-start.7
  676.9 1.8 collective-permute-start.8
  678.9 804.1 %copy-start.1 = (f32[4,40,128]{2,1,0:T(8,128)S(1)}, f32[4,40,128]{2,1,0:T(8,128)}, u32[]{:S(2)}) copy-start(f32[4,40,128]{2,1,0:T(8,128)} %param.27) | copy-start | bytes 245764
  769.9 61.4 %collective-permute-start.9 = (f32[5,2,44,128]{3,2,1,0:T(8,128)S(1)}, f32[5,2,44,128]{3,2,1,0:T(8,128)S(1)}, u32[]{:S(2)}, u32[]{:S(2)}) collective-permute-start(f32[5,2,44,128]{3,2,1,0:T(8,128)S(1)} %slice.374), channel_id=1, source_target_pairs={{0,8},{8,16},{16,24},{24,32},{32,40},{40,48},{48,56},{56,64},{64,7... | collective-permute-start | bytes 675848 | tf_op jit(solution)/shard_map/ppermute | solution.py:14
  831.4 645.5 %collective-permute-start.10 = (f32[5,4,2,128]{3,2,1,0:T(2,128)S(1)}, f32[5,4,2,128]{3,2,1,0:T(2,128)S(1)}, u32[]{:S(2)}, u32[]{:S(2)}) collective-permute-start(f32[5,4,2,128]{3,2,1,0:T(2,128)S(1)} %get-tuple-element.514), channel_id=1, source_target_pairs={{0,1},{1,2},{2,3},{3,4},{4,5},{5,6},{6,7},{7,0},{8,9},{9,10},{10,1... | collective-permute-start | bytes 61448 | tf_op jit(solution)/shard_map/ppermute | solution.py:24
  1475.5 7.5 collective-permute-start.11
where the time goes:
time: 1490 us; the launch traced here: 1480 us
  starting transfers between devices  1280 us (86%)
  other arithmetic  156 us (10%)
  waiting for transfers between devices  27.1 us (2%)
  local copies, waits for them, and re-layouts  16.1 us (1%)
    ppermute x4, starting transfers between devices, padded(): before = lax.ppermute(last, axis, up)  1160 us
    ppermute x4, starting transfers between devices, from_behind(): return lax.ppermute(value, axis, pairs)  109 us
    reduce_sum x3, other arithmetic, descreen_tile(): jnp.sum(weights * hct_integral(distance, away[1][:, None, :], home[2][:,...  45.2 us
    reduce_sum x6, other arithmetic, separation(): return (separations, jnp.sum(separations * separations, axis=0))  31 us
  transfers between devices with their start and end apart: 12, of which 11 were waited for; matrix products, arithmetic and copies ran while one was open for 1% of the time, Pallas kernels for 0%

commit v1 on v0

v1 whole, which is shorter than its diff:
```python
import functools

import jax
import jax.numpy as jnp
import numpy as np
from jax import lax
from jax.experimental import pallas as pl
from jax.experimental.pallas import tpu as pltpu
from jax.sharding import PartitionSpec as P

dielectric_factor = 1.0 - 1.0 / 78.5
radius_offset = 0.09
block_side = 8.0
log2e = 1.4426950408889634
ln2 = 0.6931471805599453
f32 = jnp.float32
bf16 = jnp.bfloat16

near_steps = ((0, 1), (1, -1), (1, 0), (1, 1))
far_steps = ((0, 2), (1, -2), (1, 2), (2, -2), (2, -1), (2, 0), (2, 1), (2, 2))
all_steps = near_steps + far_steps


def series_coefficients():
    top = (0.85 * 1.91 / 9.0) ** 2 * 1.001
    nodes = 0.5 * top * (1.0 + np.cos(np.pi * (np.arange(4) + 0.5) / 4))
    exact = sum(2.0 * (k + 1) / (2 * k + 3) * nodes**k for k in range(40))
    return [float(c) for c in np.polynomial.polynomial.polyfit(nodes, exact, 3)]


series = series_coefficients()
chunk = 64


def step_tables():
    scale = np.ones((13, 8))
    shift = np.zeros((13, 8))
    scale[12, 5:8] = 0.0
    for k, (ox, oy) in enumerate(all_steps):
        scale[k, 5:8] = (16 * ox, 16 * oy, 64 * (ox * ox + oy * oy))
        shift[k, 0:2] = (8 * ox, 8 * oy)
    none = np.zeros_like(shift)
    scale = np.concatenate([scale] * 6, axis=1)
    shift = np.concatenate([shift, none, shift, none, none, shift], axis=1)
    tables = np.stack([scale, shift])[..., None] * np.ones(128)
    return jnp.asarray(tables, bf16)


def from_behind(value, axis, steps):
    count = lax.axis_size(axis)
    pairs = [(source, (source + steps) % count) for source in range(count)]
    return lax.ppermute(value, axis, pairs)


def padded(array, sides, width):
    for axis, dim in sides:
        count, length = (lax.axis_size(axis), array.shape[dim])
        up = [(i, (i + 1) % count) for i in range(count)]
        down = [(j, i) for i, j in up]
        last = lax.slice_in_dim(array, length - width, length, axis=dim)
        leading = lax.slice_in_dim(array, 0, width, axis=dim)
        before = lax.ppermute(last, axis, up)
        after = lax.ppermute(leading, axis, down)
        array = jnp.concatenate([before, array, after], axis=dim)
    return array


def atom_terms(atom_type, type_radius, type_scale):
    type_hits = (atom_type[..., None] == jnp.arange(type_radius.shape[0], dtype=jnp.int32)).astype(
        jnp.float32
    )
    radius = jnp.sum(type_hits * type_radius, axis=-1)
    inner_radius = radius - radius_offset
    scaled = jnp.sum(type_hits * type_scale, axis=-1) * inner_radius
    return (radius, inner_radius, scaled)


def split3(value):
    first = value.astype(bf16).astype(f32)
    rest = value - first
    second = rest.astype(bf16).astype(f32)
    return first, second, rest - second


def dot(a, b, ca, cb):
    return lax.dot_general(a, b, (((ca,), (cb,)), ((), ())), preferred_element_type=f32)


def sublane(shape=(8, 128)):
    return lax.broadcasted_iota(jnp.int32, shape, 0)


def squared_length(xyz):
    square = xyz * xyz
    return jnp.sum(square, axis=0, keepdims=True)


def centred(raw):
    row = sublane()
    middle = jnp.where(row < 2, 4.0, 8.0)
    return jnp.where(row < 3, raw - middle, 0.0)


def away_operand(xyz):
    length = squared_length(xyz)
    row = sublane()
    value = jnp.where(row < 3, xyz, jnp.where(row == 4, length, 1.0))
    value = jnp.where(row == 5, xyz[0:1], jnp.where(row == 6, xyz[1:2], value))
    step = jnp.where(row == 4, 2.0, 4.0)
    first = jnp.round(value * step) * (1.0 / step)
    rest = value - first
    second = rest.astype(bf16).astype(f32)
    third = rest - second
    return jnp.concatenate([first, second, first, second, third, first], axis=0).astype(bf16)


def home_operand(xyz, factor):
    length = squared_length(xyz)
    row = sublane()
    value = jnp.where(row < 3, -2.0 * xyz, jnp.where(row == 3, length, 1.0)) * factor
    first, second, third = split3(value)
    stacked = jnp.concatenate([first, first, second, second, first, third], axis=0)
    return jnp.transpose(stacked).astype(bf16)


def lanes_of(rows, k):
    return jnp.broadcast_to(rows[:, k : k + 1], (128, 128))


def fold(value):
    return jnp.sum(value.reshape(-1, 8, 128), axis=0)


def row_totals(value, eye):
    return fold(jnp.sum(value, axis=1, keepdims=True) * eye)


def close_integral(distance, inverse, a, s, whole):
    quarter, log_factor = 0.25 * inverse, (0.5 * ln2) * inverse
    outer = distance + s
    span = distance - s
    inner = jnp.maximum(jnp.abs(span) if whole else span, a)
    inner = jnp.minimum(inner, outer)
    inv_outer = 1.0 / outer
    inv_inner = 1.0 / inner
    part = (inv_inner - inv_outer) * (
        1.0 - (outer * span) * quarter * (inv_inner + inv_outer)
    )
    total = part + log_factor * (jnp.log2(inner) - jnp.log2(outer))
    if whole:
        total = total + 2.0 * (1.0 / a - 1.0 / jnp.maximum(a, -span))
    return total


def descreen_kernel(
    dims, mask_ref, flag_ref, raw_ref, table_ref, out_ref, away_ref, near_ref, even_sq, odd_sq, even_cols, odd_cols, acc_ref
):
    rows_x, rows_y = dims
    width = rows_y + 4
    slots = (rows_x + 2) * width
    homes = rows_x * rows_y

    def prepare(slot):
        raw = raw_ref[slot]
        xyz = centred(raw)
        away_ref[slot] = away_operand(xyz)
        out_ref[slot] = jnp.zeros((8, 128), f32)
        s = raw[4:5]
        sq = s * s
        cube = s * sq
        near_ref[slot] = jnp.concatenate(
            [raw[3:5], series[0] * cube, series[1] * cube * sq, series[2] * cube * (sq * sq), series[3] * cube * (sq * sq) * sq, jnp.zeros((2, 128), f32)], axis=0
        )

    def prepare_turn(n, carry):
        for k in range(4):
            prepare(4 * n + k)
        return carry

    lax.fori_loop(0, slots // 4, prepare_turn, 0)
    eye = (
        lax.broadcasted_iota(jnp.int32, (128, 128), 0)
        == lax.broadcasted_iota(jnp.int32, (128, 128), 1)
    ).astype(f32)

    def slot_of(n):
        block_x = n // rows_y
        return block_x * width + 2 + (n - block_x * rows_y)

    def distances(n, sq_ref, cols_ref):
        slot = slot_of(n)
        left = home_operand(centred(raw_ref[slot]), 1.0)
        sq_ref[:, 12 * 128 : 13 * 128] = dot(left, away_ref[slot] * table_ref[0, 12], 1, 0)
        for k0 in range(0, 12, 2):
            right = []
            for k in (k0, k0 + 1):
                there = slot + all_steps[k][0] * width + all_steps[k][1]
                right.append(away_ref[there] * table_ref[0, k] + table_ref[1, k])
            sq_ref[:, 128 * k0 : 128 * k0 + 256] = dot(left, jnp.concatenate(right, axis=1), 1, 0)
        columns = jnp.transpose(near_ref[slot])
        for k in range(6):
            cols_ref[k] = lanes_of(columns, k)

    def pairs(n, sq_ref, cols_ref, whole):
        slot = slot_of(n)
        here = near_ref[slot]
        for c in range(0, 128, chunk):
            part = pl.ds(c, chunk)
            own = sq_ref[part, 12 * 128 : 13 * 128] + eye[c : c + chunk]
            inverse = lax.rsqrt(own)
            total = close_integral(own * inverse, inverse, cols_ref[0, part], here[1:2], whole)
            acc_ref[part] = total * (1.0 - eye[c : c + chunk])
        for k in range(12):
            there = slot + all_steps[k][0] * width + all_steps[k][1]
            ox, oy = all_steps[k]
            m = mask_ref[n * 25 + (ox + 2) * 5 + oy + 2].astype(f32)
            near = near_ref[there]
            backs = 0.0
            for c in range(0, 128, chunk):
                part = pl.ds(c, chunk)
                sq = sq_ref[part, 128 * k : 128 * k + 128]
                if k < 4:
                    inverse = lax.rsqrt(sq)
                    distance = sq * inverse
                    total = close_integral(distance, inverse, cols_ref[0, part], near[1:2] * m, whole)
                    back = close_integral(distance, inverse, near[0:1] + (1.0 - m) * 1e9, cols_ref[1, part], whole)
                else:
                    rows = near * m
                    w = 1.0 / sq
                    ww = w * w
                    total = ww * (rows[2:3] + w * (rows[3:4] + w * (rows[4:5] + w * rows[5:6])))
                    back = ww * (cols_ref[2, part] + w * (cols_ref[3, part] + w * (cols_ref[4, part] + w * cols_ref[5, part])))
                acc_ref[part] += total
                backs = backs + fold(back)
            out_ref[there] += backs if k < 4 else m * backs
        out_ref[slot] += row_totals(acc_ref[...], eye)

    def turns(whole):
        distances(0, even_sq, even_cols)

        def turn(i, carry):
            n = 2 * i
            distances(n + 1, odd_sq, odd_cols)
            pairs(n, even_sq, even_cols, whole)
            distances(jnp.minimum(n + 2, homes - 1), even_sq, even_cols)
            pairs(n + 1, odd_sq, odd_cols, whole)
            return carry

        lax.fori_loop(0, homes // 2, turn, 0)

    @pl.when(flag_ref[0] == 0)
    def _():
        turns(False)

    @pl.when(flag_ref[0] != 0)
    def _():
        turns(True)


def screen_kernel(
    dims, mask_ref, raw_ref, born_ref, table_ref, away_ref, moment_ref, out_ref, rows_ref, vec_ref,
    even_sq, odd_sq, even_cols, odd_cols, even_high, odd_high, even_low, odd_low, acc_ref,
):
    rows_x, rows_y = dims
    width = rows_y + 4
    slots = (rows_x + 2) * width
    homes = rows_x * rows_y

    def prepare(slot):
        raw = raw_ref[slot]
        xyz = centred(raw)
        born = born_ref[pl.ds(slot, 1), :]
        inv = 1.0 / born
        half = lax.rsqrt(born)
        charge = raw[5:6]
        weak = charge * half
        strong = weak * inv
        block_x = slot // width
        block_y = slot - block_x * width
        x = xyz[0:1] + 8.0 * (block_x.astype(f32) - 0.5 * (rows_x + 1))
        y = xyz[1:2] + 8.0 * (block_y.astype(f32) - 0.5 * (width - 1))
        vector = jnp.concatenate([strong, strong * x, strong * y, strong * xyz[2:3]], axis=0)
        first, second, third = split3(vector)
        vec_ref[slot] = jnp.concatenate([first, second, third, jnp.zeros((4, 128), f32)], axis=0).astype(bf16)
        rows_ref[slot] = jnp.concatenate([inv, -log2e * inv, weak, jnp.zeros((5, 128), f32)], axis=0)
        out_ref[slot] = jnp.zeros((16, 128), f32)
        moment_ref[slot] = jnp.zeros((16, 128), f32)

    def prepare_turn(n, carry):
        for k in range(4):
            prepare(4 * n + k)
        return carry

    lax.fori_loop(0, slots // 4, prepare_turn, 0)
    odd_high[...] = jnp.zeros_like(odd_high)
    odd_low[...] = jnp.zeros_like(odd_low)
    eye = (
        lax.broadcasted_iota(jnp.int32, (128, 128), 0)
        == lax.broadcasted_iota(jnp.int32, (128, 128), 1)
    ).astype(f32)

    def pair_terms(scaled_sq, rows):
        t = scaled_sq * rows[0:1]
        e = 0.25 * jnp.exp2(scaled_sq * rows[1:2])
        inv = lax.rsqrt(t + e)
        cube = inv * inv * inv
        damped = e * cube
        return inv, cube - damped, damped + damped * t

    def slot_of(n):
        block_x = n // rows_y
        return block_x * width + 2 + (n - block_x * rows_y)

    def mask_of(n, k):
        ox, oy = all_steps[k]
        return mask_ref[n * 25 + (ox + 2) * 5 + oy + 2].astype(f32)

    def away_of(slot, k):
        return slot + all_steps[k][0] * width + all_steps[k][1]

    def distances(n, sq_ref, cols_ref):
        slot = slot_of(n)
        here = rows_ref[slot]
        left = home_operand(centred(raw_ref[slot]), 0.25 * here[0:1])
        cols_ref[...] = lanes_of(jnp.transpose(here), 2)
        sq_ref[:, 12 * 128 : 13 * 128] = dot(left, away_ref[slot] * table_ref[0, 12], 1, 0)
        for k0 in range(0, 12, 2):
            right = [away_ref[away_of(slot, k)] * table_ref[0, k] + table_ref[1, k] for k in (k0, k0 + 1)]
            sq_ref[:, 128 * k0 : 128 * k0 + 256] = dot(left, jnp.concatenate(right, axis=1), 1, 0)

    def pairs(n, sq_ref, cols_ref, high_ref, low_ref):
        slot = slot_of(n)
        here = rows_ref[slot]

        def keep(part, k, pull):
            high = pull.astype(bf16)
            high_ref[part, 128 * k : 128 * k + 128] = high
            low_ref[part, 128 * k : 128 * k + 128] = (pull - high.astype(f32)).astype(bf16)

        for c in range(0, 128, chunk):
            part = pl.ds(c, chunk)
            inv, pull, stretch = pair_terms(sq_ref[part, 12 * 128 : 13 * 128], here)
            off = 1.0 - eye[c : c + chunk]
            weak = off * here[2:3]
            acc_ref[0, part] = inv * weak
            acc_ref[1, part] = stretch * weak
            keep(part, 12, pull * off)
        for k in range(12):
            there = away_of(slot, k)
            rows = rows_ref[there]
            m = mask_of(n, k)
            weak = rows[2:3] * m
            near, far = 0.0, 0.0
            for c in range(0, 128, chunk):
                part = pl.ds(c, chunk)
                inv, pull, stretch = pair_terms(sq_ref[part, 128 * k : 128 * k + 128], rows)
                acc_ref[0, part] += inv * weak
                acc_ref[1, part] += stretch * weak
                near = near + fold(inv * cols_ref[part])
                far = far + fold(stretch * cols_ref[part])
                keep(part, k, pull)
            out_ref[there, 0:8] += m * near
            out_ref[there, 8:16] += m * far
        out_ref[slot, 0:8] += row_totals(acc_ref[0], eye)
        out_ref[slot, 8:16] += row_totals(acc_ref[1], eye)

    def moments(n, high_ref, low_ref):
        slot = slot_of(n)
        own = vec_ref[slot]
        own = jnp.concatenate([own, own], axis=1)
        vectors = [vec_ref[away_of(slot, k)] * mask_of(n, k).astype(bf16) for k in range(12)] + [vec_ref[slot]]
        totals = dot(high_ref[...], jnp.concatenate(vectors, axis=1), 1, 1)
        totals = totals + dot(low_ref[...], jnp.concatenate(vectors, axis=1), 1, 1)
        for k0 in range(0, 12, 2):
            lanes = slice(128 * k0, 128 * k0 + 256)
            back = dot(own, jnp.concatenate([high_ref[:, lanes], low_ref[:, lanes]], axis=0), 1, 0)
            for t in range(2):
                moment_ref[away_of(slot, k0 + t)] += mask_of(n, k0 + t) * back[:, 128 * t : 128 * t + 128]
        moment_ref[slot] += jnp.transpose(totals)

    distances(0, even_sq, even_cols)

    def turn(i, carry):
        n = 2 * i
        distances(n + 1, odd_sq, odd_cols)
        moments(jnp.maximum(n - 1, 0), odd_high, odd_low)
        pairs(n, even_sq, even_cols, even_high, even_low)
        distances(jnp.minimum(n + 2, homes - 1), even_sq, even_cols)
        moments(n, even_high, even_low)
        pairs(n + 1, odd_sq, odd_cols, odd_high, odd_low)
        return carry

    lax.fori_loop(0, homes // 2, turn, 0)
    moments(homes - 1, odd_high, odd_low)


def descreen(dims, mask, flag, raw, table):
    slots = raw.shape[0]
    smem = pl.BlockSpec(memory_space=pltpu.SMEM)
    vmem = pl.BlockSpec(memory_space=pltpu.VMEM)
    return pl.pallas_call(
        functools.partial(descreen_kernel, dims),
        out_shape=(
            jax.ShapeDtypeStruct((slots, 8, 128), f32),
            jax.ShapeDtypeStruct((slots, 48, 128), bf16),
        ),
        in_specs=[smem, smem, vmem, vmem],
        out_specs=(vmem, vmem),
        scratch_shapes=[
            pltpu.VMEM((slots, 8, 128), f32),
            pltpu.VMEM((128, 13 * 128), f32),
            pltpu.VMEM((128, 13 * 128), f32),
            pltpu.VMEM((6, 128, 128), f32),
            pltpu.VMEM((6, 128, 128), f32),
            pltpu.VMEM((128, 128), f32),
        ],
        compiler_params=pltpu.CompilerParams(vmem_limit_bytes=56 * 2**20),
        name="descreen",
    )(mask, flag, raw, table)


def screen(dims, mask, raw, born, table, away):
    slots = raw.shape[0]
    smem = pl.BlockSpec(memory_space=pltpu.SMEM)
    vmem = pl.BlockSpec(memory_space=pltpu.VMEM)
    return pl.pallas_call(
        functools.partial(screen_kernel, dims),
        out_shape=(
            jax.ShapeDtypeStruct((slots, 16, 128), f32),
            jax.ShapeDtypeStruct((slots, 16, 128), f32),
        ),
        in_specs=[smem, vmem, vmem, vmem, vmem],
        out_specs=(vmem, vmem),
        scratch_shapes=[
            pltpu.VMEM((slots, 8, 128), f32),
            pltpu.VMEM((slots, 16, 128), bf16),
            pltpu.VMEM((128, 13 * 128), f32),
            pltpu.VMEM((128, 13 * 128), f32),
            pltpu.VMEM((128, 128), f32),
            pltpu.VMEM((128, 128), f32),
            pltpu.VMEM((128, 13 * 128), bf16),
            pltpu.VMEM((128, 13 * 128), bf16),
            pltpu.VMEM((128, 13 * 128), bf16),
            pltpu.VMEM((128, 13 * 128), bf16),
            pltpu.VMEM((2, 128, 128), f32),
        ],
        compiler_params=pltpu.CompilerParams(vmem_limit_bytes=56 * 2**20),
        name="screen",
    )(mask, raw, born, table, away)


def fold_columns(columns, rows_y):
    folded = columns[:, :, 4 : rows_y + 4]
    folded = folded.at[:, :, 0:2].add(columns[:, :, 0:2])
    folded = folded.at[:, :, rows_y - 2 : rows_y].add(columns[:, :, rows_y + 6 : rows_y + 8])
    return folded


def settle(extended, rows_x, rows_y):
    arriving = from_behind(extended[:, rows_x : rows_x + 2], "gx", 1)
    middle = extended[:, 0:rows_x].at[:, 0:2].add(arriving)
    columns = padded(middle, (("gy", 2),), 2)
    return fold_columns(columns, rows_y)


def body(offsets, charges, atom_type, type_radius, type_scale, tile_mask):
    rows_x, rows_y, atoms = charges.shape
    width = rows_y + 4
    slots = (rows_x + 2) * width
    radius, inner_radius, scaled = atom_terms(atom_type, type_radius, type_scale)
    zero = jnp.zeros_like(charges)
    payload = jnp.stack([offsets[0], offsets[1], offsets[2], inner_radius, scaled, charges], axis=2)
    widened = padded(payload, (("gy", 1),), 2)
    ahead = from_behind(widened[0:2], "gx", -1)
    raw = jnp.concatenate([widened, ahead], axis=0).reshape(slots, 6, atoms)
    raw = jnp.concatenate([raw, jnp.zeros((slots, 2, atoms), f32)], axis=1)
    mask = tile_mask.reshape(-1)
    type_inner = type_radius - radius_offset
    flag = (jnp.max(type_scale * type_inner) - 0.99 > jnp.min(type_inner)).astype(jnp.int32)[None]
    table = step_tables()
    dims = (rows_x, rows_y)
    sums, away = descreen(dims, mask, flag, raw, table)
    sums = jnp.sum(sums, axis=1).reshape(1, rows_x + 2, width, atoms)
    descreen_sum = settle(sums, rows_x, rows_y)[0]
    descreen_psi = 0.5 * inner_radius * descreen_sum
    born_radius = 1.0 / (
        1.0 / inner_radius
        - jnp.tanh(descreen_psi * (1.0 - 0.8 * descreen_psi + 4.85 * descreen_psi * descreen_psi))
        / radius
    )
    born_wide = padded(born_radius, (("gy", 1),), 2)
    born_next = from_behind(born_wide[0:2], "gx", -1)
    born_ext = jnp.concatenate([born_wide, born_next], axis=0).reshape(slots, atoms)

    raw_moments, raw_sums = screen(dims, mask, raw, born_ext, table, away)
    half = lax.rsqrt(born_ext)
    weak = raw[:, 5] * half
    strong = weak / born_ext
    slot = jnp.arange(slots, dtype=jnp.int32)[:, None]
    x = raw[:, 0] - 4.0 + 8.0 * ((slot // width).astype(f32) - 0.5 * (rows_x + 1))
    y = raw[:, 1] - 4.0 + 8.0 * ((slot % width).astype(f32) - 0.5 * (width - 1))
    z = raw[:, 2] - 8.0
    moments = [raw_moments[:, k] + raw_moments[:, 4 + k] + raw_moments[:, 8 + k] for k in range(4)]
    scale = (-dielectric_factor / 8.0) * strong
    pair_sum = jnp.stack(
        [
            scale * (x * moments[0] - moments[1]),
            scale * (y * moments[0] - moments[2]),
            scale * (z * moments[0] - moments[3]),
            (-0.25 * dielectric_factor) * weak * jnp.sum(raw_sums[:, 0:8], axis=1),
            (0.25 * dielectric_factor) * strong * jnp.sum(raw_sums[:, 8:16], axis=1),
        ],
        axis=0,
    ).reshape(5, rows_x + 2, width, atoms)
    pair_sum = settle(pair_sum, rows_x, rows_y)
    charge_sq = charges * charges
    force = pair_sum[0:3]
    atom_energy = pair_sum[3] - 0.5 * dielectric_factor * charge_sq / born_radius
    born_grad = pair_sum[4] + 0.5 * dielectric_factor * charge_sq / (born_radius * born_radius)
    return (born_radius, atom_energy, force, born_grad)


def solution(mesh):
    placed = (
        P(None, "gx", "gy", None),
        P("gx", "gy", None),
        P("gx", "gy", None),
        P(),
        P(),
        P("gx", "gy", None),
    )
    return jax.shard_map(
        body,
        mesh=mesh,
        in_specs=placed,
        out_specs=(
            P("gx", "gy", None),
            P("gx", "gy", None),
            P(None, "gx", "gy", None),
            P("gx", "gy", None),
        ),
        check_vma=False,
    )
```

time: 1490 us -> 420 us (0.28)
  starting transfers between devices: 1280 us -> 18.3 us
  Pallas kernels: 0 us -> 342 us
  other arithmetic: 156 us -> 13.3 us
    ppermute x4, starting transfers between devices: 1160 us -> 4.05 us  [padded(): before = lax.ppermute(last, axis, up)]
    pallas_call x0 -> x2, Pallas kernels: none -> 342 us  [the longest x1 194 us: screen(): pl.pallas_call(functools.partial(screen_kernel, dims), out_shape=(jax.Sha...]
    reduce_sum x16 -> x2, other arithmetic: 135 us -> 2.02 us  [the longest x1 1.5 us: body(): sums = jnp.sum(sums, axis=1).reshape(1, rows_x + 2, width, atoms)]
    ppermute x4, starting transfers between devices: 109 us -> 3.59 us  [from_behind(): return lax.ppermute(value, axis, pairs)]
  transfers between devices with their start and end apart: 12 -> 12, of which waited for: 11 -> 12; matrix products, arithmetic and copies ran while one was open for 1% -> 1% of each run, Pallas kernels for 0% -> 0%
where the time goes in v1:
time: 420 us; the launch traced here: 419 us
  Pallas kernels  342 us (81%)
  waiting for transfers between devices  35.1 us (8%)
  starting transfers between devices  18.3 us (4%)
  other arithmetic  13.3 us (3%)
  local copies, waits for them, and re-layouts  7.78 us (2%)
    pallas_call x1, Pallas kernels, screen(): pl.pallas_call(functools.partial(screen_kernel, dims), out_shape=(jax.Sha...  194 us
    pallas_call x1, Pallas kernels, descreen(): pl.pallas_call(functools.partial(descreen_kernel, dims), out_shape=(jax.S...  148 us
    ppermute x4, waiting for transfers between devices, from_behind(): return lax.ppermute(value, axis, pairs)  16.4 us
    ppermute x4, waiting for transfers between devices, padded(): after = lax.ppermute(leading, axis, down)  12.3 us
    ppermute x4, starting transfers between devices, padded(): after = lax.ppermute(leading, axis, down)  10.7 us
  transfers between devices with their start and end apart: 12, of which 12 were waited for; matrix products, arithmetic and copies ran while one was open for 1% of the time, Pallas kernels for 0%

profile of v1, /device:TPU:30, one launch (start us, length us, event | category | flops | bytes accessed | tf_op | source)
XLA Modules:
  0.0 419.0 jit_solution(7077469662246572216)
XLA Ops:
  0.7 0.9 bitcast_dynamic-update-slice_fusion.4
  1.6 0.9 bitcast_dynamic-update-slice_fusion.3
  2.5 0.9 bitcast_dynamic-update-slice_fusion.2
  3.4 1.7 select_reduce_fusion
  5.1 0.9 bitcast_dynamic-update-slice_fusion
  6.0 1.2 collective-permute-start
  7.2 2.4 collective-permute-start.1
  9.6 1.8 collective-permute-done
  11.4 3.3 collective-permute-done.1
  14.7 3.3 collective-permute-start.2
  18.0 0.6 add_reduce_fusion
  20.0 0.1 copy.34
  20.1 0.8 reshape.697.mask_ref
  20.9 1.4 collective-permute-done.2
  22.3 0.1 pad_maximum_fusion
  22.4 0.5 copy.35
  22.9 1.2 concatenate.63.raw_ref
  24.0 148.0 %descreen.1 = (f32[264,8,128]{2,1,0:T(8,128)}, bf16[264,48,128]{2,1,0:T(8,128)(2,1)}) custom-call(s32[4000]{0:T(1024)} %reshape.697.mask_ref, s32[1]{0:T(128)} %bitcast.flag_ref, f32[264,8,128]{2,1,0:T(8,128)} %concatenate.63.raw_ref, bf16[2,13,48,128]{3,2,1,0:T(8,128)(2,1)} %constant.214.clone.table_ref), custom_call_target="tpu_custom_call" | custom-call | tf_op jit(solution)/shard_map/descreen/pallas_call | solution.py:401
  172.1 1.5 reduce_sum.54
  173.6 0.1 collective-permute-start.3
  173.7 5.8 %collective-permute-done.3 = f32[1,2,44,128]{3,2,1,0:T(8,128)S(1)} collective-permute-done((f32[1,2,44,128]{3,2,1,0:T(8,128)S(1)}, f32[1,2,44,128]{3,2,1,0:T(8,128)S(1)}, u32[]{:S(2)}, u32[]{:S(2)}) %collective-permute-start.3) | collective-permute-done | bytes 45088 | tf_op jit(solution)/shard_map/ppermute | solution.py:52
  179.5 1.9 collective-permute-start.4
  181.5 1.7 collective-permute-start.5
  183.2 1.5 collective-permute-done.4
  184.7 4.1 collective-permute-done.5
  188.8 0.1 broadcast_divide_fusion
  188.9 0.3 collective-permute-start.6
  189.1 3.5 collective-permute-start.7
  192.7 1.6 collective-permute-done.6
  194.2 2.2 collective-permute-done.7
  196.5 0.1 collective-permute-start.8
  196.6 0.4 slice_add_fusion.1
  197.0 1.3 collective-permute-done.8
  198.3 0.7 reshape.700.born_ref
  199.0 194.3 %screen.1 = (f32[264,16,128]{2,1,0:T(8,128)}, f32[264,16,128]{2,1,0:T(8,128)}) custom-call(s32[4000]{0:T(1024)} %reshape.697.mask_ref, f32[264,8,128]{2,1,0:T(8,128)} %concatenate.63.raw_ref, f32[264,128]{1,0:T(8,128)} %reshape.700.born_ref, bf16[2,13,48,128]{3,2,1,0:T(8,128)(2,1)} %constant.214.clone.table_ref, bf16[264,48,128]{2,1,0:T(8,128)(2,1)} %get-tuple-element.81.away_ref), custom_call_target="tpu_custom_call" | custom-call | tf_op jit(solution)/shard_map/screen/pallas_call | solution.py:426
  393.2 7.1 %slice_add_fusion.4 = (f32[264,1,128]{2,1,0:T(1,128)S(1)}, f32[264,1,128]{2,1,0:T(1,128)S(1)}, f32[264,1,128]{2,1,0:T(1,128)S(1)}, f32[264,1,128]{2,1,0:T(1,128)S(1)}) fusion(f32[264,16,128]{2,1,0:T(8,128)} %get-tuple-element.82), kind=kLoop, calls=%fused_computation.32 | loop fusion | flops 270336 | bytes 2162688 | tf_op jit(solution)/shard_map/add | solution.py:503
  400.3 0.5 slice_reduce_fusion
  400.9 0.1 fusion.7
  401.0 0.1 fusion.4
  401.1 0.1 fusion.2
  401.3 0.1 collective-permute-start.9
  401.4 7.9 %collective-permute-done.9 = f32[5,2,44,128]{3,2,1,0:T(8,128)S(1)} collective-permute-done((f32[5,2,44,128]{3,2,1,0:T(8,128)S(1)}, f32[5,2,44,128]{3,2,1,0:T(8,128)S(1)}, u32[]{:S(2)}, u32[]{:S(2)}) %collective-permute-start.9) | collective-permute-done | bytes 225312 | tf_op jit(solution)/shard_map/ppermute | solution.py:52
  409.4 0.6 collective-permute-start.10
  410.1 3.1 collective-permute-start.11
  413.1 1.6 collective-permute-done.10
  414.8 2.7 collective-permute-done.11
  417.6 0.7 fusion.15
  418.3 0.7 slice.370
  (42 shorter events, 0.5 us)
Async XLA Ops:
  0.6 17.4 %copy-start.4 = (f32[16]{0:T(128)S(1)}, f32[16]{0:T(128)}, u32[]{:S(2)}) copy-start(f32[16]{0:T(128)} %param.23) | copy-start | bytes 196
  0.6 17.4 %copy-start.5 = (f32[16]{0:T(128)S(1)}, f32[16]{0:T(128)}, u32[]{:S(2)}) copy-start(f32[16]{0:T(128)} %param.22) | copy-start | bytes 196
  0.7 19.3 %copy-start.3 = (s32[4,40,25]{1,0,2:T(4,128)S(1)}, s32[4,40,25]{1,0,2:T(4,128)}, u32[]{:S(2)}) copy-start(s32[4,40,25]{1,0,2:T(4,128)} %param.24) | copy-start | bytes 48004
  6.0 5.4 %collective-permute-start = (f32[4,2,6,128]{3,1,0,2:T(2,128)S(1)}, f32[4,2,6,128]{3,1,0,2:T(2,128)S(1)}, u32[]{:S(2)}, u32[]{:S(2)}) collective-permute-start(f32[4,2,6,128]{3,1,0,2:T(2,128)S(1)} %get-tuple-element.104), channel_id=1, source_target_pairs={{0,1},{1,2},{2,3},{3,4},{4,5},{5,6},{6,7},{7,0},{8,9},{9,10},{10,1... | collective-permute-start | bytes 73736 | tf_op jit(solution)/shard_map/ppermute | solution.py:62
  7.2 7.4 %collective-permute-start.1 = (f32[4,2,6,128]{3,1,0,2:T(2,128)S(1)}, f32[4,2,6,128]{3,1,0,2:T(2,128)S(1)}, u32[]{:S(2)}, u32[]{:S(2)}) collective-permute-start(f32[4,2,6,128]{3,1,0,2:T(2,128)S(1)} %get-tuple-element.105), channel_id=1, source_target_pairs={{1,0},{2,1},{3,2},{4,3},{5,4},{6,5},{7,6},{0,7},{9,8},{10,9},{11,1... | collective-permute-start | bytes 73736 | tf_op jit(solution)/shard_map/ppermute | solution.py:63
  14.7 7.6 %collective-permute-start.2 = (f32[2,44,6,128]{3,1,0,2:T(8,128)S(1)}, f32[2,44,6,128]{3,1,0,2:T(8,128)S(1)}, u32[]{:S(2)}, u32[]{:S(2)}) collective-permute-start(f32[2,44,6,128]{3,1,0,2:T(8,128)S(1)} %pad_maximum_fusion.1), channel_id=1, source_target_pairs={{0,248},{8,0},{16,8},{24,16},{32,24},{40,32},{48,40},{56,48},{64,5... | collective-permute-start | bytes 811016 | tf_op jit(solution)/shard_map/ppermute | solution.py:52
  173.6 5.9 %collective-permute-start.3 = (f32[1,2,44,128]{3,2,1,0:T(8,128)S(1)}, f32[1,2,44,128]{3,2,1,0:T(8,128)S(1)}, u32[]{:S(2)}, u32[]{:S(2)}) collective-permute-start(f32[1,2,44,128]{3,2,1,0:T(8,128)S(1)} %slice.348), channel_id=1, source_target_pairs={{0,8},{8,16},{16,24},{24,32},{32,40},{40,48},{48,56},{56,64},{64,7... | collective-permute-start | bytes 135176 | tf_op jit(solution)/shard_map/ppermute | solution.py:52
  179.5 5.2 %collective-permute-start.4 = (f32[1,4,2,128]{3,2,1,0:T(2,128)S(1)}, f32[1,4,2,128]{3,2,1,0:T(2,128)S(1)}, u32[]{:S(2)}, u32[]{:S(2)}) collective-permute-start(f32[1,4,2,128]{3,2,1,0:T(2,128)S(1)} %get-tuple-element.107), channel_id=1, source_target_pairs={{0,1},{1,2},{2,3},{3,4},{4,5},{5,6},{6,7},{7,0},{8,9},{9,10},{10,1... | collective-permute-start | bytes 12296 | tf_op jit(solution)/shard_map/ppermute | solution.py:62
  181.5 7.3 %collective-permute-start.5 = (f32[1,4,2,128]{3,2,1,0:T(2,128)S(1)}, f32[1,4,2,128]{3,2,1,0:T(2,128)S(1)}, u32[]{:S(2)}, u32[]{:S(2)}) collective-permute-start(f32[1,4,2,128]{3,2,1,0:T(2,128)S(1)} %get-tuple-element.106), channel_id=1, source_target_pairs={{1,0},{2,1},{3,2},{4,3},{5,4},{6,5},{7,6},{0,7},{9,8},{10,9},{11,1... | collective-permute-start | bytes 12296 | tf_op jit(solution)/shard_map/ppermute | solution.py:63
  188.8 228.7 %copy-start.1 = (f32[4,40,128]{2,1,0:T(8,128)}, f32[4,40,128]{2,1,0:T(8,128)S(1)}, u32[]{:S(2)}) copy-start(f32[4,40,128]{2,1,0:T(8,128)S(1)} %broadcast_divide_fusion) | copy-start | bytes 245764
  188.9 5.4 %collective-permute-start.6 = (f32[4,2,128]{2,1,0:T(2,128)S(1)}, f32[4,2,128]{2,1,0:T(2,128)S(1)}, u32[]{:S(2)}, u32[]{:S(2)}) collective-permute-start(f32[4,2,128]{2,1,0:T(2,128)S(1)} %get-tuple-element.110), channel_id=1, source_target_pairs={{0,1},{1,2},{2,3},{3,4},{4,5},{5,6},{6,7},{7,0},{8,9},{9,10},{10,1... | collective-permute-start | bytes 12296 | tf_op jit(solution)/shard_map/ppermute | solution.py:62
  189.1 7.3 %collective-permute-start.7 = (f32[4,2,128]{2,1,0:T(2,128)S(1)}, f32[4,2,128]{2,1,0:T(2,128)S(1)}, u32[]{:S(2)}, u32[]{:S(2)}) collective-permute-start(f32[4,2,128]{2,1,0:T(2,128)S(1)} %get-tuple-element.111), channel_id=1, source_target_pairs={{1,0},{2,1},{3,2},{4,3},{5,4},{6,5},{7,6},{0,7},{9,8},{10,9},{11,1... | collective-permute-start | bytes 12296 | tf_op jit(solution)/shard_map/ppermute | solution.py:63
  196.5 1.8 collective-permute-start.8
  393.2 7.1 %copy-start = (f32[264,16,128]{2,1,0:T(8,128)S(1)}, f32[264,16,128]{2,1,0:T(8,128)}, u32[]{:S(2)}) copy-start(f32[264,16,128]{2,1,0:T(8,128)} %get-tuple-element.83) | copy-start | bytes 6488068
  401.3 16.3 %copy-start.2 = (f32[4,40,128]{2,1,0:T(8,128)S(1)}, f32[4,40,128]{2,1,0:T(8,128)}, u32[]{:S(2)}) copy-start(f32[4,40,128]{2,1,0:T(8,128)} %param.20) | copy-start | bytes 245764
  401.3 8.1 %collective-permute-start.9 = (f32[5,2,44,128]{3,2,1,0:T(8,128)S(1)}, f32[5,2,44,128]{3,2,1,0:T(8,128)S(1)}, u32[]{:S(2)}, u32[]{:S(2)}) collective-permute-start(f32[5,2,44,128]{3,2,1,0:T(8,128)S(1)} %slice.363), channel_id=1, source_target_pairs={{0,8},{8,16},{16,24},{24,32},{32,40},{40,48},{48,56},{56,64},{64,7... | collective-permute-start | bytes 675848 | tf_op jit(solution)/shard_map/ppermute | solution.py:52
  409.4 5.4 %collective-permute-start.10 = (f32[5,4,2,128]{3,2,1,0:T(2,128)S(1)}, f32[5,4,2,128]{3,2,1,0:T(2,128)S(1)}, u32[]{:S(2)}, u32[]{:S(2)}) collective-permute-start(f32[5,4,2,128]{3,2,1,0:T(2,128)S(1)} %get-tuple-element.103), channel_id=1, source_target_pairs={{0,1},{1,2},{2,3},{3,4},{4,5},{5,6},{6,7},{7,0},{8,9},{9,10},{10,1... | collective-permute-start | bytes 61448 | tf_op jit(solution)/shard_map/ppermute | solution.py:62
  410.1 7.5 %collective-permute-start.11 = (f32[5,4,2,128]{3,2,1,0:T(2,128)S(1)}, f32[5,4,2,128]{3,2,1,0:T(2,128)S(1)}, u32[]{:S(2)}, u32[]{:S(2)}) collective-permute-start(f32[5,4,2,128]{3,2,1,0:T(2,128)S(1)} %get-tuple-element.102), channel_id=1, source_target_pairs={{1,0},{2,1},{3,2},{4,3},{5,4},{6,5},{7,6},{0,7},{9,8},{10,9},{11,1... | collective-permute-start | bytes 61448 | tf_op jit(solution)/shard_map/ppermute | solution.py:63

commit v2 on v1

--- a/solution.py
+++ b/solution.py
@@ -46,35 +46,6 @@
     return jnp.asarray(tables, bf16)
 
 
-def from_behind(value, axis, steps):
-    count = lax.axis_size(axis)
-    pairs = [(source, (source + steps) % count) for source in range(count)]
-    return lax.ppermute(value, axis, pairs)
-
-
-def padded(array, sides, width):
-    for axis, dim in sides:
-        count, length = (lax.axis_size(axis), array.shape[dim])
-        up = [(i, (i + 1) % count) for i in range(count)]
-        down = [(j, i) for i, j in up]
-        last = lax.slice_in_dim(array, length - width, length, axis=dim)
-        leading = lax.slice_in_dim(array, 0, width, axis=dim)
-        before = lax.ppermute(last, axis, up)
-        after = lax.ppermute(leading, axis, down)
-        array = jnp.concatenate([before, array, after], axis=dim)
-    return array
-
-
-def atom_terms(atom_type, type_radius, type_scale):
-    type_hits = (atom_type[..., None] == jnp.arange(type_radius.shape[0], dtype=jnp.int32)).astype(
-        jnp.float32
-    )
-    radius = jnp.sum(type_hits * type_radius, axis=-1)
-    inner_radius = radius - radius_offset
-    scaled = jnp.sum(type_hits * type_scale, axis=-1) * inner_radius
-    return (radius, inner_radius, scaled)
-
-
 def split3(value):
     first = value.astype(bf16).astype(f32)
     rest = value - first
@@ -135,21 +106,29 @@
     return fold(jnp.sum(value, axis=1, keepdims=True) * eye)
 
 
-def close_integral(distance, inverse, a, s, whole):
-    quarter, log_factor = 0.25 * inverse, (0.5 * ln2) * inverse
+def close_integral(distance, quarter, log_factor, a, s, whole):
     outer = distance + s
     span = distance - s
     inner = jnp.maximum(jnp.abs(span) if whole else span, a)
     inner = jnp.minimum(inner, outer)
     inv_outer = 1.0 / outer
     inv_inner = 1.0 / inner
-    part = (inv_inner - inv_outer) * (
-        1.0 - (outer * span) * quarter * (inv_inner + inv_outer)
-    )
-    total = part + log_factor * (jnp.log2(inner) - jnp.log2(outer))
+    ratio = outer * inv_inner
+    total = (inv_inner - inv_outer) * (1.0 - (span * quarter) * (ratio + 1.0))
+    total = total + log_factor * jnp.log2(ratio)
     if whole:
         total = total + 2.0 * (1.0 / a - 1.0 / jnp.maximum(a, -span))
     return total
+
+
+def weave(*parts):
+    live = list(parts)
+    while live:
+        for part in list(live):
+            for _ in range(2 if part is parts[-1] and len(parts) > 1 else 1):
+                if next(part, live) is live:
+                    live.remove(part)
+                    break
 
 
 def descreen_kernel(
@@ -190,16 +169,19 @@
     def distances(n, sq_ref, cols_ref):
         slot = slot_of(n)
         left = home_operand(centred(raw_ref[slot]), 1.0)
+        columns = jnp.transpose(near_ref[slot])
         sq_ref[:, 12 * 128 : 13 * 128] = dot(left, away_ref[slot] * table_ref[0, 12], 1, 0)
+        cols_ref[0] = lanes_of(columns, 0)
+        yield
         for k0 in range(0, 12, 2):
             right = []
             for k in (k0, k0 + 1):
                 there = slot + all_steps[k][0] * width + all_steps[k][1]
                 right.append(away_ref[there] * table_ref[0, k] + table_ref[1, k])
             sq_ref[:, 128 * k0 : 128 * k0 + 256] = dot(left, jnp.concatenate(right, axis=1), 1, 0)
-        columns = jnp.transpose(near_ref[slot])
-        for k in range(6):
-            cols_ref[k] = lanes_of(columns, k)
+            if k0 < 10:
+                cols_ref[k0 // 2 + 1] = lanes_of(columns, k0 // 2 + 1)
+            yield
 
     def pairs(n, sq_ref, cols_ref, whole):
         slot = slot_of(n)
@@ -208,8 +190,9 @@
             part = pl.ds(c, chunk)
             own = sq_ref[part, 12 * 128 : 13 * 128] + eye[c : c + chunk]
             inverse = lax.rsqrt(own)
-            total = close_integral(own * inverse, inverse, cols_ref[0, part], here[1:2], whole)
+            total = close_integral(own * inverse, 0.25 * inverse, (-0.5 * ln2) * inverse, cols_ref[0, part], here[1:2], whole)
             acc_ref[part] = total * (1.0 - eye[c : c + chunk])
+        yield
         for k in range(12):
             there = slot + all_steps[k][0] * width + all_steps[k][1]
             ox, oy = all_steps[k]
@@ -222,8 +205,9 @@
                 if k < 4:
                     inverse = lax.rsqrt(sq)
                     distance = sq * inverse
-                    total = close_integral(distance, inverse, cols_ref[0, part], near[1:2] * m, whole)
-                    back = close_integral(distance, inverse, near[0:1] + (1.0 - m) * 1e9, cols_ref[1, part], whole)
+                    scales = (0.25 * inverse, (-0.5 * ln2) * inverse)
+                    total = close_integral(distance, *scales, cols_ref[0, part], near[1:2] * m, whole)
+                    back = close_integral(distance, *scales, near[0:1] + (1.0 - m) * 1e9, cols_ref[1, part], whole)
                 else:
                     rows = near * m
                     w = 1.0 / sq
@@ -233,17 +217,20 @@
                 acc_ref[part] += total
                 backs = backs + fold(back)
             out_ref[there] += backs if k < 4 else m * backs
+            yield
         out_ref[slot] += row_totals(acc_ref[...], eye)
+        yield
 
     def turns(whole):
-        distances(0, even_sq, even_cols)
+        weave(distances(0, even_sq, even_cols))
 
         def turn(i, carry):
             n = 2 * i
-            distances(n + 1, odd_sq, odd_cols)
-            pairs(n, even_sq, even_cols, whole)
-            distances(jnp.minimum(n + 2, homes - 1), even_sq, even_cols)
-            pairs(n + 1, odd_sq, odd_cols, whole)
+            weave(distances(n + 1, odd_sq, odd_cols), pairs(n, even_sq, even_cols, whole))
+            weave(
+                distances(jnp.minimum(n + 2, homes - 1), even_sq, even_cols),
+                pairs(n + 1, odd_sq, odd_cols, whole),
+            )
             return carry
 
         lax.fori_loop(0, homes // 2, turn, 0)
@@ -269,7 +256,7 @@
     def prepare(slot):
         raw = raw_ref[slot]
         xyz = centred(raw)
-        born = born_ref[pl.ds(slot, 1), :]
+        born = born_ref[slot]
         inv = 1.0 / born
         half = lax.rsqrt(born)
         charge = raw[5:6]
@@ -324,9 +311,11 @@
         left = home_operand(centred(raw_ref[slot]), 0.25 * here[0:1])
         cols_ref[...] = lanes_of(jnp.transpose(here), 2)
         sq_ref[:, 12 * 128 : 13 * 128] = dot(left, away_ref[slot] * table_ref[0, 12], 1, 0)
+        yield
         for k0 in range(0, 12, 2):
             right = [away_ref[away_of(slot, k)] * table_ref[0, k] + table_ref[1, k] for k in (k0, k0 + 1)]
             sq_ref[:, 128 * k0 : 128 * k0 + 256] = dot(left, jnp.concatenate(right, axis=1), 1, 0)
+            yield
 
     def pairs(n, sq_ref, cols_ref, high_ref, low_ref):
         slot = slot_of(n)
@@ -345,6 +334,7 @@
             acc_ref[0, part] = inv * weak
             acc_ref[1, part] = stretch * weak
             keep(part, 12, pull * off)
+        yield
         for k in range(12):
             there = away_of(slot, k)
             rows = rows_ref[there]
@@ -361,37 +351,51 @@
                 keep(part, k, pull)
             out_ref[there, 0:8] += m * near
             out_ref[there, 8:16] += m * far
+            yield
         out_ref[slot, 0:8] += row_totals(acc_ref[0], eye)
         out_ref[slot, 8:16] += row_totals(acc_ref[1], eye)
+        yield
 
     def moments(n, high_ref, low_ref):
         slot = slot_of(n)
         own = vec_ref[slot]
         own = jnp.concatenate([own, own], axis=1)
         vectors = [vec_ref[away_of(slot, k)] * mask_of(n, k).astype(bf16) for k in range(12)] + [vec_ref[slot]]
-        totals = dot(high_ref[...], jnp.concatenate(vectors, axis=1), 1, 1)
-        totals = totals + dot(low_ref[...], jnp.concatenate(vectors, axis=1), 1, 1)
+        totals = 0.0
         for k0 in range(0, 12, 2):
             lanes = slice(128 * k0, 128 * k0 + 256)
             back = dot(own, jnp.concatenate([high_ref[:, lanes], low_ref[:, lanes]], axis=0), 1, 0)
             for t in range(2):
                 moment_ref[away_of(slot, k0 + t)] += mask_of(n, k0 + t) * back[:, 128 * t : 128 * t + 128]
+            if k0 % 4 == 2:
+                group = slice(k0 - 2, k0 + 3 if k0 == 10 else k0 + 2)
+                lanes = slice(128 * group.start, 128 * group.stop)
+                totals = totals + dot(
+                    jnp.concatenate([high_ref[:, lanes], low_ref[:, lanes]], axis=1),
+                    jnp.concatenate(vectors[group] * 2, axis=1), 1, 1,
+                )
+            yield
         moment_ref[slot] += jnp.transpose(totals)
-
-    distances(0, even_sq, even_cols)
+        yield
+
+    weave(distances(0, even_sq, even_cols))
 
     def turn(i, carry):
-        n = 2 * i
-        distances(n + 1, odd_sq, odd_cols)
-        moments(jnp.maximum(n - 1, 0), odd_high, odd_low)
-        pairs(n, even_sq, even_cols, even_high, even_low)
-        distances(jnp.minimum(n + 2, homes - 1), even_sq, even_cols)
-        moments(n, even_high, even_low)
-        pairs(n + 1, odd_sq, odd_cols, odd_high, odd_low)
+        for n in (4 * i, 4 * i + 2):
+            weave(
+                distances(n + 1, odd_sq, odd_cols),
+                moments(jnp.maximum(n - 1, 0), odd_high, odd_low),
+                pairs(n, even_sq, even_cols, even_high, even_low),
+            )
+            weave(
+                distances(jnp.minimum(n + 2, homes - 1), even_sq, even_cols),
+                moments(n, even_high, even_low),
+                pairs(n + 1, odd_sq, odd_cols, odd_high, odd_low),
+            )
         return carry
 
-    lax.fori_loop(0, homes // 2, turn, 0)
-    moments(homes - 1, odd_high, odd_low)
+    lax.fori_loop(0, homes // 4, turn, 0)
+    weave(moments(homes - 1, odd_high, odd_low))
 
 
 def descreen(dims, mask, flag, raw, table):
@@ -449,75 +453,217 @@
     )(mask, raw, born, table, away)
 
 
-def fold_columns(columns, rows_y):
-    folded = columns[:, :, 4 : rows_y + 4]
-    folded = folded.at[:, :, 0:2].add(columns[:, :, 0:2])
-    folded = folded.at[:, :, rows_y - 2 : rows_y].add(columns[:, :, rows_y + 6 : rows_y + 8])
-    return folded
-
-
-def settle(extended, rows_x, rows_y):
-    arriving = from_behind(extended[:, rows_x : rows_x + 2], "gx", 1)
-    middle = extended[:, 0:rows_x].at[:, 0:2].add(arriving)
-    columns = padded(middle, (("gy", 2),), 2)
-    return fold_columns(columns, rows_y)
+def around(dx, dy):
+    count_x, count_y = lax.axis_size("gx"), lax.axis_size("gy")
+    return (
+        lax.rem(lax.axis_index("gx") + (dx + count_x), count_x),
+        lax.rem(lax.axis_index("gy") + (dy + count_y), count_y),
+    )
+
+
+def greet():
+    barrier = pltpu.get_barrier_semaphore()
+    ring = [(dx, dy) for dx in (-1, 0, 1) for dy in (-1, 0, 1) if (dx, dy) != (0, 0)]
+    for dx, dy in ring:
+        pl.semaphore_signal(barrier, inc=1, device_id=around(dx, dy), device_id_type=pl.DeviceIdType.MESH)
+    pl.semaphore_wait(barrier, len(ring))
+
+
+def send(src, dst, sems, k, to):
+    copy = pltpu.make_async_remote_copy(
+        src_ref=src,
+        dst_ref=dst,
+        send_sem=sems.at[0, k],
+        recv_sem=sems.at[1, k],
+        device_id=around(*to),
+        device_id_type=pl.DeviceIdType.MESH,
+    )
+    copy.start()
+    return copy
+
+
+def fill_halo(ext, sems, rows_x, rows_y):
+    own = pl.ds(2, rows_y)
+    top, ahead = pl.ds(0, 2), pl.ds(rows_x, 2)
+    body_rows = pl.ds(0, rows_x)
+    left, first = pl.ds(0, 2), pl.ds(2, 2)
+    last, right = pl.ds(rows_y, 2), pl.ds(rows_y + 2, 2)
+    plan = [
+        (top, own, ahead, own, (-1, 0)),
+        (body_rows, last, body_rows, left, (0, 1)),
+        (body_rows, first, body_rows, right, (0, -1)),
+        (top, last, ahead, left, (-1, 1)),
+        (top, first, ahead, right, (-1, -1)),
+    ]
+    copies = [
+        send(ext.at[rs, cs], ext.at[rd, cd], sems, k, to)
+        for k, (rs, cs, rd, cd, to) in enumerate(plan)
+    ]
+    for copy in copies:
+        copy.wait()
+
+
+def give_back(ext, ahead_land, side_land, corner_land, sems, rows_x, rows_y):
+    own = pl.ds(2, rows_y)
+    ahead, body_rows = pl.ds(rows_x, 2), pl.ds(0, rows_x)
+    left, right = pl.ds(0, 2), pl.ds(rows_y + 2, 2)
+    copies = [
+        send(ext.at[ahead, own], ahead_land, sems, 0, (1, 0)),
+        send(ext.at[body_rows, left], side_land.at[0], sems, 1, (0, -1)),
+        send(ext.at[body_rows, right], side_land.at[1], sems, 2, (0, 1)),
+        send(ext.at[ahead, left], corner_land.at[0], sems, 3, (1, -1)),
+        send(ext.at[ahead, right], corner_land.at[1], sems, 4, (1, 1)),
+    ]
+    for copy in copies:
+        copy.wait()
+    ext[0:2, 2 : rows_y + 2] += ahead_land[...]
+    ext[0:rows_x, rows_y : rows_y + 2] += side_land[0]
+    ext[0:rows_x, 2:4] += side_land[1]
+    ext[0:2, rows_y : rows_y + 2] += corner_land[0]
+    ext[0:2, 2:4] += corner_land[1]
+
+
+def gather_kernel(radius_ref, scale_ref, offsets_ref, charge_ref, type_ref, ext, sems):
+    rows_x, rows_y, _ = charge_ref.shape
+    greet()
+    for x in range(rows_x):
+        for y in range(0, rows_y, 8):
+            types = type_ref[x, y : y + 8]
+            radius = jnp.zeros((8, 128), f32)
+            scale = jnp.zeros((8, 128), f32)
+            for k in range(radius_ref.shape[0]):
+                radius = jnp.where(types == k, radius_ref[k], radius)
+                scale = jnp.where(types == k, scale_ref[k], scale)
+            inner = radius - radius_offset
+            parts = [offsets_ref[k, x, y : y + 8] for k in range(3)]
+            parts += [inner, scale * inner, charge_ref[x, y : y + 8], radius, jnp.zeros((8, 128), f32)]
+            for k, part in enumerate(parts):
+                ext[x, 2 + y : 10 + y, k, :] = part
+    fill_halo(ext, sems, rows_x, rows_y)
+
+
+def born_kernel(sum_ref, raw_ref, born_ref, ext, ahead_land, side_land, corner_land, sems):
+    width = sum_ref.shape[1]
+    rows_x, rows_y = sum_ref.shape[0] - 2, width - 4
+    greet()
+
+    def reduce_turn(x, carry):
+        for y in range(width):
+            ext[x, y] = jnp.sum(sum_ref[x, y], axis=0, keepdims=True)
+        return carry
+
+    lax.fori_loop(0, rows_x + 2, reduce_turn, 0)
+    give_back(ext, ahead_land, side_land, corner_land, sems.at[0], rows_x, rows_y)
+
+    def radius_turn(x, carry):
+        for y in range(2, rows_y + 2):
+            raw = raw_ref[x, y]
+            inner, radius = raw[3:4], raw[6:7]
+            psi = 0.5 * inner * ext[x, y]
+            bent = jnp.tanh(psi * (1.0 - 0.8 * psi + 4.85 * psi * psi))
+            born_ref[x, y] = 1.0 / (1.0 / inner - bent / radius)
+        return carry
+
+    lax.fori_loop(0, rows_x, radius_turn, 0)
+    fill_halo(born_ref, sems.at[1], rows_x, rows_y)
+
+
+def settle_kernel(
+    moment_ref, sum_ref, raw_ref, born_ref, born_out, energy_out, force_out, grad_out,
+    ext, ahead_land, side_land, corner_land, sems,
+):
+    width = sum_ref.shape[1]
+    rows_x, rows_y = sum_ref.shape[0] - 2, width - 4
+    greet()
+    row = sublane()
+
+    def finish_turn(x, carry):
+        for y in range(width):
+            raw = raw_ref[x, y]
+            born = born_ref[x, y]
+            inv = 1.0 / born
+            weak = raw[5:6] * lax.rsqrt(born)
+            strong = weak * inv
+            moment = moment_ref[x, y]
+            moment = moment[0:8] + moment[8:16]
+            moment = moment[0:4] + moment[4:8]
+            middle = jnp.where(row == 0, 8.0 * (x.astype(f32) - 0.5 * (rows_x + 1)) - 4.0, 8.0 * (y - 0.5 * (width - 1)) - 4.0)
+            place = raw + jnp.where(row == 2, -8.0, middle)
+            force = ((-dielectric_factor / 8.0) * strong) * (place[0:3] * moment[0:1] - moment[1:4])
+            sums = sum_ref[x, y]
+            energy = ((-0.25 * dielectric_factor) * weak) * jnp.sum(sums[0:8], axis=0, keepdims=True)
+            grad = ((0.25 * dielectric_factor) * strong) * jnp.sum(sums[8:16], axis=0, keepdims=True)
+            ext[x, y] = jnp.concatenate([force, energy, grad, jnp.zeros((3, 128), f32)], axis=0)
+        return carry
+
+    lax.fori_loop(0, rows_x + 2, finish_turn, 0)
+    give_back(ext, ahead_land, side_land, corner_land, sems, rows_x, rows_y)
+    for x in range(rows_x):
+        for y in range(0, rows_y, 8):
+            here = slice(2 + y, 10 + y)
+            there = slice(y, y + 8)
+            born = born_ref[x, here, 0, :]
+            charge = raw_ref[x, here, 5, :]
+            own = (0.5 * dielectric_factor) * (charge * charge) / born
+            born_out[x, there] = born
+            for k in range(3):
+                force_out[k, x, there] = ext[x, here, k, :]
+            energy_out[x, there] = ext[x, here, 3, :] - own
+            grad_out[x, there] = ext[x, here, 4, :] + own / born
+
+
+def exchange(kernel, ident, ins, outs, scratch):
+    smem = pl.BlockSpec(memory_space=pltpu.SMEM)
+    vmem = pl.BlockSpec(memory_space=pltpu.VMEM)
+    return pl.pallas_call(
+        kernel,
+        out_shape=tuple(jax.ShapeDtypeStruct(shape, f32) for shape in outs),
+        in_specs=[smem if value.ndim == 1 else vmem for value in ins],
+        out_specs=tuple(vmem for _ in outs),
+        scratch_shapes=scratch,
+        compiler_params=pltpu.CompilerParams(
+            collective_id=ident, has_side_effects=True, vmem_limit_bytes=56 * 2**20
+        ),
+        name=kernel.__name__,
+    )(*ins)
+
+
+def landing(rows_x, rows_y, depth):
+    return [
+        pltpu.VMEM((rows_x + 2, rows_y + 4, depth, 128), f32),
+        pltpu.VMEM((2, rows_y, depth, 128), f32),
+        pltpu.VMEM((2, rows_x, 2, depth, 128), f32),
+        pltpu.VMEM((2, 2, 2, depth, 128), f32),
+    ]
 
 
 def body(offsets, charges, atom_type, type_radius, type_scale, tile_mask):
     rows_x, rows_y, atoms = charges.shape
-    width = rows_y + 4
-    slots = (rows_x + 2) * width
-    radius, inner_radius, scaled = atom_terms(atom_type, type_radius, type_scale)
-    zero = jnp.zeros_like(charges)
-    payload = jnp.stack([offsets[0], offsets[1], offsets[2], inner_radius, scaled, charges], axis=2)
-    widened = padded(payload, (("gy", 1),), 2)
-    ahead = from_behind(widened[0:2], "gx", -1)
-    raw = jnp.concatenate([widened, ahead], axis=0).reshape(slots, 6, atoms)
-    raw = jnp.concatenate([raw, jnp.zeros((slots, 2, atoms), f32)], axis=1)
+    dims = (rows_x, rows_y)
+    grid = (rows_x + 2, rows_y + 4)
+    slots = grid[0] * grid[1]
+    dma = pltpu.SemaphoreType.DMA
+    (raw,) = exchange(
+        gather_kernel, 0, (type_radius, type_scale, offsets, charges, atom_type),
+        [grid + (8, atoms)], [dma((2, 5))],
+    )
     mask = tile_mask.reshape(-1)
     type_inner = type_radius - radius_offset
     flag = (jnp.max(type_scale * type_inner) - 0.99 > jnp.min(type_inner)).astype(jnp.int32)[None]
     table = step_tables()
-    dims = (rows_x, rows_y)
-    sums, away = descreen(dims, mask, flag, raw, table)
-    sums = jnp.sum(sums, axis=1).reshape(1, rows_x + 2, width, atoms)
-    descreen_sum = settle(sums, rows_x, rows_y)[0]
-    descreen_psi = 0.5 * inner_radius * descreen_sum
-    born_radius = 1.0 / (
-        1.0 / inner_radius
-        - jnp.tanh(descreen_psi * (1.0 - 0.8 * descreen_psi + 4.85 * descreen_psi * descreen_psi))
-        / radius
+    raw_slots = raw.reshape(slots, 8, atoms)
+    sums, away = descreen(dims, mask, flag, raw_slots, table)
+    (born,) = exchange(
+        born_kernel, 1, (sums.reshape(grid + (8, atoms)), raw),
+        [grid + (1, atoms)], landing(rows_x, rows_y, 1) + [dma((2, 2, 5))],
     )
-    born_wide = padded(born_radius, (("gy", 1),), 2)
-    born_next = from_behind(born_wide[0:2], "gx", -1)
-    born_ext = jnp.concatenate([born_wide, born_next], axis=0).reshape(slots, atoms)
-
-    raw_moments, raw_sums = screen(dims, mask, raw, born_ext, table, away)
-    half = lax.rsqrt(born_ext)
-    weak = raw[:, 5] * half
-    strong = weak / born_ext
-    slot = jnp.arange(slots, dtype=jnp.int32)[:, None]
-    x = raw[:, 0] - 4.0 + 8.0 * ((slot // width).astype(f32) - 0.5 * (rows_x + 1))
-    y = raw[:, 1] - 4.0 + 8.0 * ((slot % width).astype(f32) - 0.5 * (width - 1))
-    z = raw[:, 2] - 8.0
-    moments = [raw_moments[:, k] + raw_moments[:, 4 + k] + raw_moments[:, 8 + k] for k in range(4)]
-    scale = (-dielectric_factor / 8.0) * strong
-    pair_sum = jnp.stack(
-        [
-            scale * (x * moments[0] - moments[1]),
-            scale * (y * moments[0] - moments[2]),
-            scale * (z * moments[0] - moments[3]),
-            (-0.25 * dielectric_factor) * weak * jnp.sum(raw_sums[:, 0:8], axis=1),
-            (0.25 * dielectric_factor) * strong * jnp.sum(raw_sums[:, 8:16], axis=1),
-        ],
-        axis=0,
-    ).reshape(5, rows_x + 2, width, atoms)
-    pair_sum = settle(pair_sum, rows_x, rows_y)
-    charge_sq = charges * charges
-    force = pair_sum[0:3]
-    atom_energy = pair_sum[3] - 0.5 * dielectric_factor * charge_sq / born_radius
-    born_grad = pair_sum[4] + 0.5 * dielectric_factor * charge_sq / (born_radius * born_radius)
-    return (born_radius, atom_energy, force, born_grad)
+    moments, pair_sums = screen(dims, mask, raw_slots, born.reshape(slots, 1, atoms), table, away)
+    shape = (rows_x, rows_y, atoms)
+    return exchange(
+        settle_kernel, 2,
+        (moments.reshape(grid + (16, atoms)), pair_sums.reshape(grid + (16, atoms)), raw, born),
+        [shape, shape, (3,) + shape, shape], landing(rows_x, rows_y, 8) + [dma((2, 5))],
+    )
 
 
 def solution(mesh):

time: 420 us -> 386 us (0.919)
  waiting for transfers between devices: 35.1 us -> 0 us
  Pallas kernels: 342 us -> 371 us
  starting transfers between devices: 18.3 us -> 0 us
  other arithmetic: 13.3 us -> 1.28 us
    pallas_call x0 -> x3, Pallas kernels: none -> 49.8 us  [exchange(): pl.pallas_call(kernel, out_shape=tuple((jax.ShapeDtypeStruct(shape, f32)...]
    ppermute x12 -> x0, waiting for transfers between devices: 35.1 us -> none  [the longest x4 16.4 us: from_behind(): return lax.ppermute(value, axis, pairs)]
    ppermute x12 -> x0, starting transfers between devices: 18.3 us -> none  [the longest x4 10.7 us: padded(): after = lax.ppermute(leading, axis, down)]
    pallas_call x1, Pallas kernels: 194 us -> 179 us  [screen(): pl.pallas_call(functools.partial(screen_kernel, dims), out_shape=(jax.Sha...]
    add x2 -> x0, other arithmetic: 7.8 us -> none  [the longest x1 7.07 us: body(): raw_moments[:, k] + raw_moments[:, 4 + k] + raw_moments[:, 8 + k]]
    pallas_call x1, Pallas kernels: 148 us -> 142 us  [descreen(): pl.pallas_call(functools.partial(descreen_kernel, dims), out_shape=(jax.S...]
    unnamed x17 -> x5, local copies, waits for them, and re-layouts: 2.85 us -> 7.13 us
  transfers between devices with their start and end apart: 12 -> 0, of which waited for: 12 -> 0; matrix products, arithmetic and copies ran while one was open for 1% -> 0% of each run, Pallas kernels for 0% -> 0%
where the time goes in v2:
time: 386 us; the launch traced here: 382 us
  Pallas kernels  371 us (96%)
  local copies, waits for them, and re-layouts  7.94 us (2%)
    pallas_call x1, Pallas kernels, screen(): pl.pallas_call(functools.partial(screen_kernel, dims), out_shape=(jax.Sha...  179 us
    pallas_call x1, Pallas kernels, descreen(): pl.pallas_call(functools.partial(descreen_kernel, dims), out_shape=(jax.S...  142 us
    pallas_call x3, Pallas kernels, exchange(): pl.pallas_call(kernel, out_shape=tuple((jax.ShapeDtypeStruct(shape, f32)...  49.8 us

profile of v2, /device:TPU:30, one launch (start us, length us, event | category | flops | bytes accessed | tf_op | source)
XLA Modules:
  0.0 382.3 jit_solution(7010998323742638250)
XLA Ops:
  0.6 1.3 add_reduce_fusion
  3.2 0.9 copy.11
  4.1 0.8 reshape.26.mask_ref
  4.9 14.3 %gather_kernel.1.raw_ref = f32[6,44,8,128]{3,2,1,0:T(8,128)} custom-call(f32[16]{0:T(128)} %radius_ref.1, f32[16]{0:T(128)} %scale_ref.1, f32[3,4,40,128]{3,2,1,0:T(8,128)} %offsets_ref.1, f32[4,40,128]{2,1,0:T(8,128)} %charge_ref.1, s32[4,40,128]{2,1,0:T(8,128)} %type_ref.1), custom_call_target="tpu_custom_call" | custom-call | tf_op jit(solution)/shard_map/gather_kernel/pallas_call | solution.py:618
  19.2 142.1 %descreen.1 = (f32[264,8,128]{2,1,0:T(8,128)}, bf16[264,48,128]{2,1,0:T(8,128)(2,1)}) custom-call(s32[4000]{0:T(1024)} %reshape.26.mask_ref, s32[1]{0:T(128)} %bitcast.1.flag_ref, f32[264,8,128]{2,1,0:T(8,128)} %bitcast.6, bf16[2,13,48,128]{3,2,1,0:T(8,128)(2,1)} %constant.12.clone.table_ref), custom_call_target="tpu_custom_call" | custom-call | tf_op jit(solution)/shard_map/descreen/pallas_call | solution.py:405
  161.4 18.1 %born_kernel.1.born_ref = f32[6,44,1,128]{3,2,1,0:T(1,128)} custom-call(f32[6,44,8,128]{3,2,1,0:T(8,128)} %bitcast.11, f32[6,44,8,128]{3,2,1,0:T(8,128)} %gather_kernel.1.raw_ref), custom_call_target="tpu_custom_call" | custom-call | tf_op jit(solution)/shard_map/born_kernel/pallas_call | solution.py:618
  179.4 179.1 %screen.1 = (f32[264,16,128]{2,1,0:T(8,128)}, f32[264,16,128]{2,1,0:T(8,128)}) custom-call(s32[4000]{0:T(1024)} %reshape.26.mask_ref, f32[264,8,128]{2,1,0:T(8,128)} %bitcast.7, f32[264,1,128]{2,1,0:T(1,128)} %bitcast.10, bf16[2,13,48,128]{3,2,1,0:T(8,128)(2,1)} %constant.12.clone.table_ref, bf16[264,48,128]{2,1,0:T(8,128)(2,1)} %get-tuple-element.9.away_ref), custom_call_target="tpu_custom_call" | custom-call | tf_op jit(solution)/shard_map/screen/pallas_call | solution.py:430
  358.6 17.4 %settle_kernel.1 = (f32[4,40,128]{2,1,0:T(8,128)}, f32[4,40,128]{2,1,0:T(8,128)}, f32[3,4,40,128]{3,2,1,0:T(8,128)}, f32[4,40,128]{2,1,0:T(8,128)}) custom-call(f32[6,44,16,128]{3,2,1,0:T(8,128)} %bitcast.8, f32[6,44,16,128]{3,2,1,0:T(8,128)} %bitcast.9, f32[6,44,8,128]{3,2,1,0:T(8,128)} %gather_kernel.1.raw_ref, f32[6,44,1,128]{3,2,1,0:T(1,128)} %born_kernel.1.born_ref), custom_call_target="tpu_custom_call" | custom-call | tf_op jit(solution)/shard_map/settle_kernel/pallas_call | solution.py:618
  376.0 1.5 copy.16
  377.5 1.5 copy.17
  379.1 1.7 copy.18
  380.7 1.5 copy.19

commit v3 on v2

--- a/solution.py
+++ b/solution.py
@@ -132,7 +132,7 @@
 
 
 def descreen_kernel(
-    dims, mask_ref, flag_ref, raw_ref, table_ref, out_ref, away_ref, near_ref, even_sq, odd_sq, even_cols, odd_cols, acc_ref
+    dims, mask_ref, radius_ref, scale_ref, raw_ref, table_ref, out_ref, away_ref, near_ref, even_sq, odd_sq, even_cols, odd_cols, acc_ref
 ):
     rows_x, rows_y = dims
     width = rows_y + 4
@@ -235,11 +235,18 @@
 
         lax.fori_loop(0, homes // 2, turn, 0)
 
-    @pl.when(flag_ref[0] == 0)
+    least, most = radius_ref[0] - radius_offset, 0.0
+    for k in range(radius_ref.shape[0]):
+        inner = radius_ref[k] - radius_offset
+        least = jnp.minimum(least, inner)
+        most = jnp.maximum(most, scale_ref[k] * inner)
+    reached = most - 0.99 > least
+
+    @pl.when(jnp.logical_not(reached))
     def _():
         turns(False)
 
-    @pl.when(flag_ref[0] != 0)
+    @pl.when(reached)
     def _():
         turns(True)
 
@@ -367,13 +374,12 @@
             back = dot(own, jnp.concatenate([high_ref[:, lanes], low_ref[:, lanes]], axis=0), 1, 0)
             for t in range(2):
                 moment_ref[away_of(slot, k0 + t)] += mask_of(n, k0 + t) * back[:, 128 * t : 128 * t + 128]
-            if k0 % 4 == 2:
-                group = slice(k0 - 2, k0 + 3 if k0 == 10 else k0 + 2)
-                lanes = slice(128 * group.start, 128 * group.stop)
-                totals = totals + dot(
-                    jnp.concatenate([high_ref[:, lanes], low_ref[:, lanes]], axis=1),
-                    jnp.concatenate(vectors[group] * 2, axis=1), 1, 1,
-                )
+            group = slice(k0, k0 + 3 if k0 == 10 else k0 + 2)
+            lanes = slice(128 * group.start, 128 * group.stop)
+            totals = totals + dot(
+                jnp.concatenate([high_ref[:, lanes], low_ref[:, lanes]], axis=1),
+                jnp.concatenate(vectors[group] * 2, axis=1), 1, 1,
+            )
             yield
         moment_ref[slot] += jnp.transpose(totals)
         yield
@@ -381,7 +387,7 @@
     weave(distances(0, even_sq, even_cols))
 
     def turn(i, carry):
-        for n in (4 * i, 4 * i + 2):
+        for n in [16 * i + 2 * u for u in range(8)]:
             weave(
                 distances(n + 1, odd_sq, odd_cols),
                 moments(jnp.maximum(n - 1, 0), odd_high, odd_low),
@@ -394,11 +400,11 @@
             )
         return carry
 
-    lax.fori_loop(0, homes // 4, turn, 0)
+    lax.fori_loop(0, homes // 16, turn, 0)
     weave(moments(homes - 1, odd_high, odd_low))
 
 
-def descreen(dims, mask, flag, raw, table):
+def descreen(dims, mask, type_radius, type_scale, raw, table):
     slots = raw.shape[0]
     smem = pl.BlockSpec(memory_space=pltpu.SMEM)
     vmem = pl.BlockSpec(memory_space=pltpu.VMEM)
@@ -408,7 +414,7 @@
             jax.ShapeDtypeStruct((slots, 8, 128), f32),
             jax.ShapeDtypeStruct((slots, 48, 128), bf16),
         ),
-        in_specs=[smem, smem, vmem, vmem],
+        in_specs=[smem, smem, smem, vmem, vmem],
         out_specs=(vmem, vmem),
         scratch_shapes=[
             pltpu.VMEM((slots, 8, 128), f32),
@@ -420,7 +426,7 @@
         ],
         compiler_params=pltpu.CompilerParams(vmem_limit_bytes=56 * 2**20),
         name="descreen",
-    )(mask, flag, raw, table)
+    )(mask, type_radius, type_scale, raw, table)
 
 
 def screen(dims, mask, raw, born, table, away):
@@ -569,8 +575,7 @@
 
 
 def settle_kernel(
-    moment_ref, sum_ref, raw_ref, born_ref, born_out, energy_out, force_out, grad_out,
-    ext, ahead_land, side_land, corner_land, sems,
+    moment_ref, sum_ref, raw_ref, born_ref, ext, ahead_land, side_land, corner_land, sems
 ):
     width = sum_ref.shape[1]
     rows_x, rows_y = sum_ref.shape[0] - 2, width - 4
@@ -598,6 +603,10 @@
 
     lax.fori_loop(0, rows_x + 2, finish_turn, 0)
     give_back(ext, ahead_land, side_land, corner_land, sems, rows_x, rows_y)
+
+
+def finish_kernel(ext, raw_ref, born_ref, born_out, energy_out, force_out, grad_out):
+    rows_x, rows_y, _ = born_out.shape
     for x in range(rows_x):
         for y in range(0, rows_y, 8):
             here = slice(2 + y, 10 + y)
@@ -622,7 +631,7 @@
         out_specs=tuple(vmem for _ in outs),
         scratch_shapes=scratch,
         compiler_params=pltpu.CompilerParams(
-            collective_id=ident, has_side_effects=True, vmem_limit_bytes=56 * 2**20
+            collective_id=ident, has_side_effects=ident is not None, vmem_limit_bytes=56 * 2**20
         ),
         name=kernel.__name__,
     )(*ins)
@@ -648,21 +657,22 @@
         [grid + (8, atoms)], [dma((2, 5))],
     )
     mask = tile_mask.reshape(-1)
-    type_inner = type_radius - radius_offset
-    flag = (jnp.max(type_scale * type_inner) - 0.99 > jnp.min(type_inner)).astype(jnp.int32)[None]
     table = step_tables()
     raw_slots = raw.reshape(slots, 8, atoms)
-    sums, away = descreen(dims, mask, flag, raw_slots, table)
+    sums, away = descreen(dims, mask, type_radius, type_scale, raw_slots, table)
     (born,) = exchange(
         born_kernel, 1, (sums.reshape(grid + (8, atoms)), raw),
         [grid + (1, atoms)], landing(rows_x, rows_y, 1) + [dma((2, 2, 5))],
     )
     moments, pair_sums = screen(dims, mask, raw_slots, born.reshape(slots, 1, atoms), table, away)
+    (settled,) = exchange(
+        settle_kernel, 2,
+        (moments.reshape(grid + (16, atoms)), pair_sums.reshape(grid + (16, atoms)), raw, born),
+        [grid + (8, atoms)], landing(rows_x, rows_y, 8)[1:] + [dma((2, 5))],
+    )
     shape = (rows_x, rows_y, atoms)
     return exchange(
-        settle_kernel, 2,
-        (moments.reshape(grid + (16, atoms)), pair_sums.reshape(grid + (16, atoms)), raw, born),
-        [shape, shape, (3,) + shape, shape], landing(rows_x, rows_y, 8) + [dma((2, 5))],
+        finish_kernel, None, (settled, raw, born), [shape, shape, (3,) + shape, shape], []
     )
 
 

time: 386 us -> 362 us (0.938)
  Pallas kernels: 371 us -> 357 us
  local copies, waits for them, and re-layouts: 7.94 us -> 1.71 us
    pallas_call x1, Pallas kernels: 179 us -> 162 us  [screen(): pl.pallas_call(functools.partial(screen_kernel, dims), out_shape=(jax.Sha...]
    unnamed x5 -> x1, local copies, waits for them, and re-layouts: 7.13 us -> 0.9 us
    pallas_call x3 -> x4, Pallas kernels: 49.8 us -> 52.5 us  [exchange(): pl.pallas_call(kernel, out_shape=tuple((jax.ShapeDtypeStruct(shape, f32)...]
where the time goes in v3:
time: 362 us; the launch traced here: 359 us
  Pallas kernels  357 us (99%)
    pallas_call x1, Pallas kernels, screen(): pl.pallas_call(functools.partial(screen_kernel, dims), out_shape=(jax.Sha...  162 us
    pallas_call x1, Pallas kernels, descreen(): pl.pallas_call(functools.partial(descreen_kernel, dims), out_shape=(jax.S...  142 us
    pallas_call x4, Pallas kernels, exchange(): pl.pallas_call(kernel, out_shape=tuple((jax.ShapeDtypeStruct(shape, f32)...  52.5 us

profile of v3, /device:TPU:30, one launch (start us, length us, event | category | flops | bytes accessed | tf_op | source)
XLA Modules:
  0.0 358.9 jit_solution(801700732388501982)
XLA Ops:
  0.6 0.9 copy.11
  1.5 0.8 reshape.26.mask_ref
  2.3 14.3 %gather_kernel.1.raw_ref = f32[6,44,8,128]{3,2,1,0:T(8,128)} custom-call(f32[16]{0:T(128)} %radius_ref.3, f32[16]{0:T(128)} %scale_ref.3, f32[3,4,40,128]{3,2,1,0:T(8,128)} %offsets_ref.1, f32[4,40,128]{2,1,0:T(8,128)} %charge_ref.1, s32[4,40,128]{2,1,0:T(8,128)} %type_ref.1), custom_call_target="tpu_custom_call" | custom-call | tf_op jit(solution)/shard_map/gather_kernel/pallas_call | solution.py:627
  16.7 142.1 %descreen.1 = (f32[264,8,128]{2,1,0:T(8,128)}, bf16[264,48,128]{2,1,0:T(8,128)(2,1)}) custom-call(s32[4000]{0:T(1024)} %reshape.26.mask_ref, f32[16]{0:T(128)} %radius_ref.3, f32[16]{0:T(128)} %scale_ref.3, f32[264,8,128]{2,1,0:T(8,128)} %bitcast.5, bf16[2,13,48,128]{3,2,1,0:T(8,128)(2,1)} %constant.2.clone.table_ref), custom_call_target="tpu_custom_call" | custom-call | tf_op jit(solution)/shard_map/descreen/pallas_call | solution.py:411
  158.8 18.1 %born_kernel.1.born_ref = f32[6,44,1,128]{3,2,1,0:T(1,128)} custom-call(f32[6,44,8,128]{3,2,1,0:T(8,128)} %bitcast.10, f32[6,44,8,128]{3,2,1,0:T(8,128)} %gather_kernel.1.raw_ref), custom_call_target="tpu_custom_call" | custom-call | tf_op jit(solution)/shard_map/born_kernel/pallas_call | solution.py:627
  176.9 161.9 %screen.1 = (f32[264,16,128]{2,1,0:T(8,128)}, f32[264,16,128]{2,1,0:T(8,128)}) custom-call(s32[4000]{0:T(1024)} %reshape.26.mask_ref, f32[264,8,128]{2,1,0:T(8,128)} %bitcast.6, f32[264,1,128]{2,1,0:T(1,128)} %bitcast.9, bf16[2,13,48,128]{3,2,1,0:T(8,128)(2,1)} %constant.2.clone.table_ref, bf16[264,48,128]{2,1,0:T(8,128)(2,1)} %get-tuple-element.9.away_ref), custom_call_target="tpu_custom_call" | custom-call | tf_op jit(solution)/shard_map/screen/pallas_call | solution.py:436
  338.8 17.4 %settle_kernel.1.ext = f32[6,44,8,128]{3,2,1,0:T(8,128)} custom-call(f32[6,44,16,128]{3,2,1,0:T(8,128)} %bitcast.7, f32[6,44,16,128]{3,2,1,0:T(8,128)} %bitcast.8, f32[6,44,8,128]{3,2,1,0:T(8,128)} %gather_kernel.1.raw_ref, f32[6,44,1,128]{3,2,1,0:T(1,128)} %born_kernel.1.born_ref), custom_call_target="tpu_custom_call" | custom-call | tf_op jit(solution)/shard_map/settle_kernel/pallas_call | solution.py:627
  356.2 2.7 finish_kernel.1

commit v4 on v3

--- a/solution.py
+++ b/solution.py
@@ -472,7 +472,10 @@
     ring = [(dx, dy) for dx in (-1, 0, 1) for dy in (-1, 0, 1) if (dx, dy) != (0, 0)]
     for dx, dy in ring:
         pl.semaphore_signal(barrier, inc=1, device_id=around(dx, dy), device_id_type=pl.DeviceIdType.MESH)
-    pl.semaphore_wait(barrier, len(ring))
+
+
+def await_ring():
+    pl.semaphore_wait(pltpu.get_barrier_semaphore(), 8)
 
 
 def send(src, dst, sems, k, to):
@@ -545,6 +548,7 @@
             parts += [inner, scale * inner, charge_ref[x, y : y + 8], radius, jnp.zeros((8, 128), f32)]
             for k, part in enumerate(parts):
                 ext[x, 2 + y : 10 + y, k, :] = part
+    await_ring()
     fill_halo(ext, sems, rows_x, rows_y)
 
 
@@ -559,6 +563,7 @@
         return carry
 
     lax.fori_loop(0, rows_x + 2, reduce_turn, 0)
+    await_ring()
     give_back(ext, ahead_land, side_land, corner_land, sems.at[0], rows_x, rows_y)
 
     def radius_turn(x, carry):
@@ -602,6 +607,7 @@
         return carry
 
     lax.fori_loop(0, rows_x + 2, finish_turn, 0)
+    await_ring()
     give_back(ext, ahead_land, side_land, corner_land, sems, rows_x, rows_y)
 
 

time: 362 us -> 360 us (level)
  no operation moved by 1% of the time
where the time goes in v4:
time: 360 us; the launch traced here: 357 us
  Pallas kernels  354 us (98%)
    pallas_call x1, Pallas kernels, screen(): pl.pallas_call(functools.partial(screen_kernel, dims), out_shape=(jax.Sha...  162 us
    pallas_call x1, Pallas kernels, descreen(): pl.pallas_call(functools.partial(descreen_kernel, dims), out_shape=(jax.S...  142 us
    pallas_call x4, Pallas kernels, exchange(): pl.pallas_call(kernel, out_shape=tuple((jax.ShapeDtypeStruct(shape, f32)...  50.3 us

profile of v4, /device:TPU:30, one launch (start us, length us, event | category | flops | bytes accessed | tf_op | source)
XLA Modules:
  0.0 356.7 jit_solution(12194709859761671293)
XLA Ops:
  0.6 0.9 copy.11
  1.5 0.8 reshape.26.mask_ref
  2.3 13.8 %gather_kernel.1.raw_ref = f32[6,44,8,128]{3,2,1,0:T(8,128)} custom-call(f32[16]{0:T(128)} %radius_ref.3, f32[16]{0:T(128)} %scale_ref.3, f32[3,4,40,128]{3,2,1,0:T(8,128)} %offsets_ref.1, f32[4,40,128]{2,1,0:T(8,128)} %charge_ref.1, s32[4,40,128]{2,1,0:T(8,128)} %type_ref.1), custom_call_target="tpu_custom_call" | custom-call | tf_op jit(solution)/shard_map/gather_kernel/pallas_call | solution.py:633
  16.2 142.2 %descreen.1 = (f32[264,8,128]{2,1,0:T(8,128)}, bf16[264,48,128]{2,1,0:T(8,128)(2,1)}) custom-call(s32[4000]{0:T(1024)} %reshape.26.mask_ref, f32[16]{0:T(128)} %radius_ref.3, f32[16]{0:T(128)} %scale_ref.3, f32[264,8,128]{2,1,0:T(8,128)} %bitcast.5, bf16[2,13,48,128]{3,2,1,0:T(8,128)(2,1)} %constant.2.clone.table_ref), custom_call_target="tpu_custom_call" | custom-call | tf_op jit(solution)/shard_map/descreen/pallas_call | solution.py:411
  158.3 17.8 %born_kernel.1.born_ref = f32[6,44,1,128]{3,2,1,0:T(1,128)} custom-call(f32[6,44,8,128]{3,2,1,0:T(8,128)} %bitcast.10, f32[6,44,8,128]{3,2,1,0:T(8,128)} %gather_kernel.1.raw_ref), custom_call_target="tpu_custom_call" | custom-call | tf_op jit(solution)/shard_map/born_kernel/pallas_call | solution.py:633
  176.1 161.9 %screen.1 = (f32[264,16,128]{2,1,0:T(8,128)}, f32[264,16,128]{2,1,0:T(8,128)}) custom-call(s32[4000]{0:T(1024)} %reshape.26.mask_ref, f32[264,8,128]{2,1,0:T(8,128)} %bitcast.6, f32[264,1,128]{2,1,0:T(1,128)} %bitcast.9, bf16[2,13,48,128]{3,2,1,0:T(8,128)(2,1)} %constant.2.clone.table_ref, bf16[264,48,128]{2,1,0:T(8,128)(2,1)} %get-tuple-element.9.away_ref), custom_call_target="tpu_custom_call" | custom-call | tf_op jit(solution)/shard_map/screen/pallas_call | solution.py:436
  338.0 16.0 %settle_kernel.1.ext = f32[6,44,8,128]{3,2,1,0:T(8,128)} custom-call(f32[6,44,16,128]{3,2,1,0:T(8,128)} %bitcast.7, f32[6,44,16,128]{3,2,1,0:T(8,128)} %bitcast.8, f32[6,44,8,128]{3,2,1,0:T(8,128)} %gather_kernel.1.raw_ref, f32[6,44,1,128]{3,2,1,0:T(1,128)} %born_kernel.1.born_ref), custom_call_target="tpu_custom_call" | custom-call | tf_op jit(solution)/shard_map/settle_kernel/pallas_call | solution.py:633
  354.0 2.7 finish_kernel.1
